TPU v7x, 512 devices: a whole 4x4x16 slice. The times are simulated.
512 devices in a mesh: panel: 32 (over x, y, core), tile: 16 (over z).
Axes of the slice: x: 4, y: 4, z: 16, core: 2. Of those that a mesh axis runs over, the one named last changes fastest.
Arguments:
- target: float32 [8192, 2048], P('tile', 'panel'), may hold values from -6 to 6
- left_factors: bfloat16 [96, 8192, 256], P('panel', 'tile'), may hold values from -0.375 to 0.375
- right_factors: bfloat16 [96, 4, 2048, 256], P('panel', None, 'tile'), may hold values from -0.125 to 0.125
- diag_left: bfloat16 [96, 2048, 256], P('panel', 'tile'), may hold values from -1.25 to 1.25
- diag_right: bfloat16 [96, 2048, 256], P('panel', 'tile'), may hold values from -0.125 to 0.125
- tile_ranks: int32 [96, 4], P('panel'), may hold values from 64 to 256
- diag_ranks: int32 [96], P('panel'), may hold values from 64 to 256
Outputs:
- updated: float32 [8192, 2048], P('tile', 'panel')
All inputs are finite; a program needn't handle non-finite values.
Results may differ from a plain program's by a relative error of at most 0.0011.
Values may be sent and summed in bfloat16 or wider, within the bound.
No kernel may reach another device: no remote copies, remote signals or barrier semaphores. Data moves between devices by JAX's collectives and lax.ppermute only.
A program may use at most 64 MiB of HBM per device.

v0:
```python
import jax
import jax.numpy as jnp
from jax import lax
from jax.sharding import PartitionSpec as P


def shards(target, left_factors, right_factors, diag_left, diag_right, tile_ranks, diag_ranks):
    column_total, row_dev, rank = left_factors.shape
    tile_count = lax.axis_size("tile")
    tile_size = diag_left.shape[1] * tile_count
    local_tile = lax.axis_index("tile") * row_dev // tile_size
    tranks = lax.dynamic_index_in_dim(tile_ranks, local_tile, 1, keepdims=False)
    positions = jnp.arange(rank)
    partial_product = jnp.einsum(
        "jmcr,jcs->jmrs", right_factors, diag_right, preferred_element_type=jnp.float32
    )
    reduced_update = lax.psum(partial_product, "tile")
    mine = lax.dynamic_index_in_dim(reduced_update, local_tile, 1, keepdims=False)
    keep = (positions[None, :, None] < tranks[:, None, None]) & (
        positions[None, None, :] < diag_ranks[:, None, None]
    )
    core = jnp.where(keep, mine, jnp.float32(0.0)).astype(jnp.bfloat16)
    mixed = jnp.einsum(
        "jnr,jrs->njs", left_factors, core, preferred_element_type=jnp.float32
    ).astype(jnp.bfloat16)
    terms = jnp.einsum(
        "njs,jcs->nc",
        mixed,
        lax.all_gather(diag_left, "tile", axis=1, tiled=True),
        preferred_element_type=jnp.float32,
    )
    delta = lax.psum_scatter(terms, "panel", scatter_dimension=1, tiled=True)
    return target - delta


def solution(mesh):
    placed = (
        P("tile", "panel"),
        P("panel", "tile", None),
        P("panel", None, "tile", None),
        P("panel", "tile", None),
        P("panel", "tile", None),
        P("panel", None),
        P("panel"),
    )
    return jax.shard_map(
        shards, mesh=mesh, in_specs=placed, out_specs=P("tile", "panel"), check_vma=False
    )
```

profile of v0, /device:TPU:1, one launch (start us, length us, event | category | flops | bytes accessed | tf_op | source)
XLA Modules:
  0.0 242.5 jit_solution(1719777242797852214)
XLA Ops:
  6.5 0.0 copy-start
  6.5 0.0 copy-start.2
  6.5 0.0 copy-start.3
  6.5 0.0 all-gather.2.cloned.1.call-start
  6.5 0.7 all-gather.2.cloned.1.call-update
  7.3 0.0 reduce-scatter.2.cloned.1.call-start
  7.3 3.4 %fusion.10 = f32[3,4,256,256]{3,2,1,0:T(8,128)} fusion(bf16[3,4,128,256]{3,2,1,0:T(8,128)(2,1)} %param.9, bf16[3,128,256]{2,1,0:T(8,128)(2,1)} %param.11), kind=kOutput, calls=%fused_computation.8 | convolution fusion | flops 201326592 | bytes 4128768 | tf_op jit(solution)/shard_map/jmcr,jcs->jmrs/dot_general | solution.py:14
  10.8 0.0 copy-done.2
  10.8 0.2 dynamic-slice_reduce_fusion
  11.0 0.0 copy-done.3
  11.0 0.1 iota_compare_fusion
  11.0 110.7 %all-reduce.1 = bf16[3,4,256,256]{3,2,1,0:T(8,128)(2,1)S(1)} all-reduce(f32[3,4,256,256]{3,2,1,0:T(8,128)} %fusion.10), channel_id=1, replica_groups=mesh['panel'=32,'tile'=16] {'tile'}, use_global_device_ids=true, to_apply=%region_0.1 | all-reduce | flops 786432 | bytes 4718592 | tf_op jit(solution)/shard_map/psum | solution.py:17
  121.7 0.0 all-gather.2.cloned.1.call-done
  121.8 0.0 copy-done
  121.8 5.9 %convolution_bitcast_fusion = f32[512,2048]{0,1:T(8,128)} fusion(bf16[3,2048,256]{2,1,0:T(8,128)(2,1)} %all-gather.2.cloned.1.call-done, bf16[3,512,256]{2,1,0:T(8,128)(2,1)S(1)} %copy-done, bf16[3,4,256,256]{3,2,1,0:T(8,128)(2,1)S(1)} %all-reduce.1, s32[]{:T(128)S(6)} %select_n.16, pred[3,256]{1,0:T(4,128)(4,1)S(1)} %get-tuple-element.5, ...), kind=kOutput, calls=%fused_computation | convolution fusion | flops 1812725760 | bytes 8521732 | tf_op jit(solution)/shard_map/njs,jcs->nc/dot_general | solution.py:26
  127.7 0.0 copy-start.1
  127.7 0.0 reduce-scatter.2.cloned.1.call-update
  127.7 106.4 %reduce-scatter.2.cloned.1.call-done = f32[512,64]{0,1:T(8,128)} async-done(((f32[512,2048]{0,1:T(8,128)}), f32[512,64]{0,1:T(8,128)}) %reduce-scatter.2.cloned.1.call-update) | async-done | bytes 131088 | tf_op jit(solution)/shard_map/reduce_scatter | solution.py:32
  234.1 0.0 copy-done.1
  234.1 1.6 sub.8
Async XLA Ops:
  6.5 115.2 %copy-start = (bf16[3,512,256]{2,1,0:T(8,128)(2,1)S(1)}, bf16[3,512,256]{2,1,0:T(8,128)(2,1)}, u32[]{:S(2)}) copy-start(bf16[3,512,256]{2,1,0:T(8,128)(2,1)} %param.8) | copy-start | bytes 2359300
  6.5 4.2 %copy-start.2 = (s32[3,4]{1,0:T(4,128)S(1)}, s32[3,4]{1,0:T(4,128)}, u32[]{:S(2)}) copy-start(s32[3,4]{1,0:T(4,128)} %param.12) | copy-start | bytes 148
  6.5 4.4 %copy-start.3 = (s32[3]{0:T(128)S(1)}, s32[3]{0:T(128)}, u32[]{:S(2)}) copy-start(s32[3]{0:T(128)} %param.13) | copy-start | bytes 40
  6.5 115.2 %all-gather.2.cloned.1.call-start = ((), (), s32[]{:S(2)}) async-start(), calls=%async_computation.1 | async-start | bytes 3342336 | tf_op jit(solution)/shard_map/all_gather | solution.py:29
  7.3 226.8 %reduce-scatter.2.cloned.1.call-start = ((), (), s32[]{:S(2)}) async-start(), calls=%async_computation.2 | async-start | bytes 4325376 | tf_op jit(solution)/shard_map/reduce_scatter | solution.py:32
  127.7 106.4 %copy-start.1 = (f32[512,64]{0,1:T(8,128)S(1)}, f32[512,64]{0,1:T(8,128)}, u32[]{:S(2)}) copy-start(f32[512,64]{0,1:T(8,128)} %param.7) | copy-start | bytes 393220
Sparse Core Ops, SparseCore 0:
  9.4 89.2 all-gather.1
  127.8 106.2 reduce-scatter.1
where the time goes:
time: 243 us
  blocking collectives  111 us (46%)
  waiting for transfers between devices  107 us (44%)
  between operations  13.4 us (6%)
  matrix products  9.36 us (4%)
    psum x1, blocking collectives, shards(): reduced_update = lax.psum(partial_product, 'tile')  111 us
    reduce_scatter x1, waiting for transfers between devices, shards(): delta = lax.psum_scatter(terms, 'panel', scatter_dimension=1, tiled=True)  106 us
    dot_general x1, matrix products, shards(): jnp.einsum('njs,jcs->nc', mixed, lax.all_gather(diag_left, 'tile', axis=1...  5.92 us
  transfers between devices with their start and end apart: 2, of which 1 were waited for; matrix products, arithmetic and copies ran while one was open for 2% of the time, Pallas kernels for 0%

commit v1 on v0

v1 whole, which is shorter than its diff:
```python
import jax
import jax.numpy as jnp
from jax import lax
from jax.sharding import PartitionSpec as P

CORES = 2
CORE_SCALE = 1024.0


def shards(target, left_factors, right_factors, diag_left, diag_right, tile_ranks, diag_ranks):
    column_count, row_dev, rank = left_factors.shape
    piece = diag_left.shape[1]
    tile_count = lax.axis_size("tile")
    panel_count = lax.axis_size("panel")
    chip_count = panel_count // CORES
    half = piece // CORES
    tile_size = piece * tile_count
    local_tile = lax.axis_index("tile") * row_dev // tile_size
    core_id = lax.axis_index("panel") % CORES
    swap = [(p, p ^ 1) for p in range(panel_count)]
    across = [[CORES * c + a for c in range(chip_count)] for a in range(CORES)]

    kept = lax.dynamic_slice_in_dim(diag_left, core_id * half, half, 1)
    given = lax.dynamic_slice_in_dim(diag_left, (1 - core_id) * half, half, 1)
    got = lax.ppermute(given, "panel", swap)
    diag_rows = lax.all_gather(jnp.concatenate([kept, got], 0), "tile", axis=1, tiled=True)

    partial_product = jnp.einsum(
        "jmcr,jcs->jmrs", right_factors, diag_right, preferred_element_type=jnp.float32
    )
    core_sum = lax.psum((partial_product * CORE_SCALE).astype(jnp.float16), "tile")
    mine = lax.dynamic_index_in_dim(core_sum, local_tile, 1, keepdims=False)
    mine = mine.astype(jnp.float32) * (1.0 / CORE_SCALE)
    tranks = lax.dynamic_index_in_dim(tile_ranks, local_tile, 1, keepdims=False)
    positions = jnp.arange(rank)
    keep = (positions[None, :, None] < tranks[:, None, None]) & (
        positions[None, None, :] < diag_ranks[:, None, None]
    )
    core = jnp.where(keep, mine, jnp.float32(0.0)).astype(jnp.bfloat16)
    mixed = jnp.einsum(
        "jnr,jrs->jns", left_factors, core, preferred_element_type=jnp.float32
    ).astype(jnp.bfloat16)
    both = jnp.concatenate([mixed, lax.ppermute(mixed, "panel", swap)], 0)

    terms = jnp.einsum("jcs,jns->cn", diag_rows, both, preferred_element_type=jnp.float32)
    terms = terms.astype(jnp.bfloat16).reshape(chip_count, half, row_dev)
    parts = lax.all_to_all(
        terms, "panel", split_axis=0, concat_axis=0, tiled=True, axis_index_groups=across
    )
    delta = jnp.sum(parts.astype(jnp.float32), axis=0)
    return target - delta.T


def solution(mesh):
    placed = (
        P("tile", "panel"),
        P("panel", "tile", None),
        P("panel", None, "tile", None),
        P("panel", "tile", None),
        P("panel", "tile", None),
        P("panel", None),
        P("panel"),
    )
    return jax.shard_map(
        shards, mesh=mesh, in_specs=placed, out_specs=P("tile", "panel"), check_vma=False
    )
```

time: 243 us -> 148 us (0.61)
  waiting for transfers between devices: 107 us -> 2.83 us
  starting transfers between devices: 0.04 us -> 20 us
  blocking collectives: 111 us -> 99.9 us
    reduce_scatter x1 -> x0, waiting for transfers between devices: 106 us -> none  [shards(): delta = lax.psum_scatter(terms, 'panel', scatter_dimension=1, tiled=True)]
    psum x1, blocking collectives: 111 us -> 77.8 us  [shards(): lax.psum((partial_product * CORE_SCALE).astype(jnp.float16), 'tile')]
    all_to_all x0 -> x1, blocking collectives: none -> 22.1 us  [shards(): lax.all_to_all(terms, 'panel', split_axis=0, concat_axis=0, tiled=True, a...]
    ppermute x0 -> x2, starting transfers between devices: none -> 20 us  [the longest x1 11.3 us: shards(): both = jnp.concatenate([mixed, lax.ppermute(mixed, 'panel', swap)], 0)]
    ppermute x0 -> x2, waiting for transfers between devices: none -> 2.81 us  [the longest x1 1.89 us: shards(): both = jnp.concatenate([mixed, lax.ppermute(mixed, 'panel', swap)], 0)]
    dot_general x1 -> x2, matrix products: 5.92 us -> 5.4 us  [the longest x1 3.69 us: shards(): jnp.einsum('jcs,jns->cn', diag_rows, both, preferred_element_type=jnp.flo...]
  transfers between devices with their start and end apart: 2 -> 3, of which waited for: 1 -> 2; matrix products, arithmetic and copies ran while one was open for 2% -> 3% of each run, Pallas kernels for 0% -> 0%
where the time goes in v1:
time: 148 us; the launch traced here: 147 us
  blocking collectives  99.9 us (68%)
  starting transfers between devices  20 us (14%)
  between operations  13.5 us (9%)
  matrix products  6.94 us (5%)
  waiting for transfers between devices  2.83 us (2%)
  other arithmetic  2.24 us (2%)
  local copies, waits for them, and re-layouts  1.91 us (1%)
    psum x1, blocking collectives, shards(): lax.psum((partial_product * CORE_SCALE).astype(jnp.float16), 'tile')  77.8 us
    all_to_all x1, blocking collectives, shards(): lax.all_to_all(terms, 'panel', split_axis=0, concat_axis=0, tiled=True, a...  22.1 us
    ppermute x1, starting transfers between devices, shards(): both = jnp.concatenate([mixed, lax.ppermute(mixed, 'panel', swap)], 0)  11.3 us
    ppermute x1, starting transfers between devices, shards(): got = lax.ppermute(given, 'panel', swap)  8.79 us
    dot_general x1, matrix products, shards(): jnp.einsum('jcs,jns->cn', diag_rows, both, preferred_element_type=jnp.flo...  3.69 us
  transfers between devices with their start and end apart: 3, of which 2 were waited for; matrix products, arithmetic and copies ran while one was open for 3% of the time, Pallas kernels for 0%

profile of v1, /device:TPU:1, one launch (start us, length us, event | category | flops | bytes accessed | tf_op | source)
XLA Modules:
  0.0 147.3 jit_solution(1553762368766303976)
XLA Ops:
  6.5 0.0 copy-start
  6.5 0.0 all-gather.2.cloned.1.call-start
  6.5 1.0 constant_dynamic-slice_fusion.1
  7.6 8.8 %collective-permute-start = (bf16[3,64,256]{2,1,0:T(8,128)(2,1)S(1)}, bf16[3,64,256]{2,1,0:T(8,128)(2,1)S(1)}, u32[]{:S(2)}, u32[]{:S(2)}) collective-permute-start(bf16[3,64,256]{2,1,0:T(8,128)(2,1)S(1)} %get-tuple-element.6), channel_id=1, source_target_pairs={{0,16},{16,0},{32,48},{48,32},{64,80},{80,64},{96,112},{112,96},{1... | collective-permute-start | bytes 294920 | tf_op jit(solution)/shard_map/ppermute | solution.py:25
  16.4 0.9 collective-permute-done
  17.3 0.7 pad_maximum_fusion
  18.0 0.0 all-gather.2.cloned.1.call-update
  18.0 0.9 dynamic-slice_reduce_fusion
  18.9 0.7 iota_compare_fusion
  19.6 0.0 copy-done
  19.6 1.5 %multiply_convert_fusion = f16[3,4,256,256]{3,2,1,0:T(8,128)(2,1)S(1)} fusion(bf16[3,4,128,256]{3,2,1,0:T(8,128)(2,1)S(1)} %copy-done, bf16[3,128,256]{2,1,0:T(8,128)(2,1)} %param.11), kind=kOutput, calls=%fused_computation | convolution fusion | flops 202899456 | bytes 2555904 | tf_op jit(solution)/shard_map/jmcr,jcs->jmrs/dot_general | solution.py:28
  21.2 0.0 copy-start.2
  21.2 77.8 %all-reduce.1 = u32[3,4,4,8192]{3,2,1,0:T(4,128)} all-reduce(u32[3,4,4,8192]{3,2,1,0:T(4,128)S(1)} %bitcast.22), channel_id=1, replica_groups=mesh['panel'=32,'tile'=16] {'tile'}, use_global_device_ids=true, to_apply=%region_0.1.clone | all-reduce | flops 393216 | bytes 3145728 | tf_op jit(solution)/shard_map/psum | solution.py:31
  99.0 0.0 copy-done.2
  99.0 1.7 %fusion.3 = bf16[3,512,256]{1,2,0:T(8,128)(2,1)S(1)} fusion(bf16[3,512,256]{2,1,0:T(8,128)(2,1)S(1)} %copy-done.2, f16[3,4,256,256]{3,2,1,0:T(8,128)(2,1)} %bitcast.23, s32[]{:T(128)S(6)} %select_n.31, pred[3,256]{1,0:T(4,128)(4,1)S(1)} %get-tuple-element.7, pred[3,256]{1,0:T(4,128)(4,1)S(1)} %get-tuple-element.8), kind=kOutput, calls=%fused_computation.7 | convolution fusion | flops 202702848 | bytes 1967620 | tf_op jit(solution)/shard_map/jnr,jrs->jns/dot_general | solution.py:40
  100.7 11.3 %collective-permute-start.1 = (bf16[3,512,256]{1,2,0:T(8,128)(2,1)S(1)}, bf16[3,512,256]{1,2,0:T(8,128)(2,1)S(1)}, u32[]{:S(2)}, u32[]{:S(2)}) collective-permute-start(bf16[3,512,256]{1,2,0:T(8,128)(2,1)S(1)} %fusion.3), channel_id=1, source_target_pairs={{0,16},{16,0},{32,48},{48,32},{64,80},{80,64},{96,112},{112,96},{1... | collective-permute-start | bytes 2359304 | tf_op jit(solution)/shard_map/ppermute | solution.py:43
  112.0 1.9 %collective-permute-done.1 = bf16[3,512,256]{1,2,0:T(8,128)(2,1)S(1)} collective-permute-done((bf16[3,512,256]{1,2,0:T(8,128)(2,1)S(1)}, bf16[3,512,256]{1,2,0:T(8,128)(2,1)S(1)}, u32[]{:S(2)}, u32[]{:S(2)}) %collective-permute-start.1) | collective-permute-done | bytes 786464 | tf_op jit(solution)/shard_map/ppermute | solution.py:43
  113.9 0.0 all-gather.2.cloned.1.call-done
  113.9 3.7 %bitcast_convert_fusion = bf16[1024,512]{1,0:T(8,128)(2,1)S(1)} fusion(bf16[6,1024,256]{2,1,0:T(8,128)(2,1)} %all-gather.2.cloned.1.call-done, bf16[3,512,256]{1,2,0:T(8,128)(2,1)S(1)} %collective-permute-done.1, bf16[3,512,256]{1,2,0:T(8,128)(2,1)S(1)} %fusion.3), kind=kOutput, calls=%fused_computation.1 | convolution fusion | flops 1611923456 | bytes 5767168 | tf_op jit(solution)/shard_map/jcs,jns->cn/dot_general | solution.py:45
  117.6 0.0 copy-start.1
  117.6 22.1 %all_to_all.5 = bf16[16,64,512]{2,1,0:T(8,128)(2,1)S(1)} all-to-all(bf16[16,64,512]{2,1,0:T(8,128)(2,1)S(1)} %bitcast.24), channel_id=1, replica_groups={{0,32,64,96,128,160,192,224,256,288,320,352,384,416,448,480},{16,48,80,..., dimensions={0} | all-to-all | bytes 2097152 | tf_op jit(solution)/shard_map/all_to_all | solution.py:47
  139.7 0.1 convert_reduce_fusion
  139.8 0.0 copy-done.1
  139.8 0.7 bitcast_subtract_fusion
Async XLA Ops:
  6.5 13.1 %copy-start = (bf16[3,4,128,256]{3,2,1,0:T(8,128)(2,1)S(1)}, bf16[3,4,128,256]{3,2,1,0:T(8,128)(2,1)}, u32[]{:S(2)}) copy-start(bf16[3,4,128,256]{3,2,1,0:T(8,128)(2,1)} %param.9) | copy-start | bytes 2359300
  6.5 107.4 %all-gather.2.cloned.1.call-start = ((), (), s32[]{:S(2)}) async-start(), calls=%async_computation.1 | async-start | bytes 3342336 | tf_op jit(solution)/shard_map/all_gather | solution.py:26
  7.6 9.7 %collective-permute-start = (bf16[3,64,256]{2,1,0:T(8,128)(2,1)S(1)}, bf16[3,64,256]{2,1,0:T(8,128)(2,1)S(1)}, u32[]{:S(2)}, u32[]{:S(2)}) collective-permute-start(bf16[3,64,256]{2,1,0:T(8,128)(2,1)S(1)} %get-tuple-element.6), channel_id=1, source_target_pairs={{0,16},{16,0},{32,48},{48,32},{64,80},{80,64},{96,112},{112,96},{1... | collective-permute-start | bytes 294920 | tf_op jit(solution)/shard_map/ppermute | solution.py:25
  21.2 77.9 %copy-start.2 = (bf16[3,512,256]{2,1,0:T(8,128)(2,1)S(1)}, bf16[3,512,256]{2,1,0:T(8,128)(2,1)}, u32[]{:S(2)}) copy-start(bf16[3,512,256]{2,1,0:T(8,128)(2,1)} %param.8) | copy-start | bytes 2359300
  100.7 13.2 %collective-permute-start.1 = (bf16[3,512,256]{1,2,0:T(8,128)(2,1)S(1)}, bf16[3,512,256]{1,2,0:T(8,128)(2,1)S(1)}, u32[]{:S(2)}, u32[]{:S(2)}) collective-permute-start(bf16[3,512,256]{1,2,0:T(8,128)(2,1)S(1)} %fusion.3), channel_id=1, source_target_pairs={{0,16},{16,0},{32,48},{48,32},{64,80},{80,64},{96,112},{112,96},{1... | collective-permute-start | bytes 2359304 | tf_op jit(solution)/shard_map/ppermute | solution.py:43
  117.6 22.2 %copy-start.1 = (f32[512,64]{0,1:T(8,128)S(1)}, f32[512,64]{0,1:T(8,128)}, u32[]{:S(2)}) copy-start(f32[512,64]{0,1:T(8,128)} %param.7) | copy-start | bytes 393220
Sparse Core Ops, SparseCore 0:
  18.1 76.8 all-gather.1

commit v2 on v1

v2 whole, which is shorter than its diff:
```python
import functools

import jax
import jax.numpy as jnp
from jax import lax
from jax.experimental import pallas as pl
from jax.experimental.pallas import tpu as pltpu
from jax.sharding import PartitionSpec as P

CORES = 2
CORE_SCALE = 1024.0
GROUP = 8
VMEM_BYTES = 16 << 20


def mix(where, tranks, dranks, left, core, mixed):
    columns, _, rank = left.shape
    row = lax.broadcasted_iota(jnp.int32, (rank, rank), 0)
    col = lax.broadcasted_iota(jnp.int32, (rank, rank), 1)
    for j in range(columns):
        keep = (row < tranks[j, where[1]]) & (col < dranks[j])
        masked = jnp.where(keep, core[j].astype(jnp.float32), 0.0).astype(jnp.bfloat16)
        mixed[j] = lax.dot_general(
            masked, left[j], (((0,), (1,)), ((), ())), preferred_element_type=jnp.float32
        ).astype(jnp.bfloat16)


def expand(diag, mixed, out):
    columns, group, _, half, rank = diag.shape
    total = None
    for j in range(columns):
        part = jnp.dot(
            diag[j].reshape(group * half, rank), mixed[j], preferred_element_type=jnp.float32
        )
        total = part if total is None else total + part
    out[...] = total.reshape(out.shape).astype(out.dtype)


def give_kernel(where, tranks, dranks, left, core, diag, mixed, out):
    @pl.when(pl.program_id(0) == 0)
    def _():
        mix(where, tranks, dranks, left, core, mixed)

    expand(diag, mixed, out)


def keep_kernel(where, mixed, diag, out):
    expand(diag, mixed, out)


def whole(shape):
    return pl.BlockSpec(shape, lambda i, *_: (0,) * len(shape))


def shards(target, left_factors, right_factors, diag_left, diag_right, tile_ranks, diag_ranks):
    column_count, row_dev, rank = left_factors.shape
    piece = diag_left.shape[1]
    tile_count = lax.axis_size("tile")
    panel_count = lax.axis_size("panel")
    chip_count = panel_count // CORES
    half = piece // CORES
    tile_size = piece * tile_count
    local_tile = lax.axis_index("tile") * row_dev // tile_size
    core_id = lax.axis_index("panel") % CORES
    swap = [(p, p ^ 1) for p in range(panel_count)]
    across = [[CORES * c + a for c in range(chip_count)] for a in range(CORES)]

    diag_rows = lax.all_gather(diag_left, "tile", axis=1, tiled=True)
    diag_rows = diag_rows.reshape(column_count, tile_count, CORES, half, rank)

    partial_product = jnp.einsum(
        "jmcr,jcs->jmrs", right_factors, diag_right, preferred_element_type=jnp.float32
    )
    core_sum = lax.psum((partial_product * CORE_SCALE).astype(jnp.float16), "tile")
    mine = lax.dynamic_index_in_dim(core_sum, local_tile, 1, keepdims=False)
    core = (mine.astype(jnp.float32) * (1.0 / CORE_SCALE)).astype(jnp.bfloat16)

    where = jnp.stack([core_id, local_tile]).astype(jnp.int32)
    grid = (tile_count // GROUP,)
    out_spec = pl.BlockSpec((GROUP, half, row_dev), lambda i, *_: (i, 0, 0))
    flops = 2 * column_count * tile_count * half * rank * row_dev
    mixed_shape = (column_count, rank, row_dev)
    diag_block = (column_count, GROUP, 1, half, rank)

    mixed, given = pl.pallas_call(
        give_kernel,
        grid_spec=pltpu.PrefetchScalarGridSpec(
            num_scalar_prefetch=3,
            grid=grid,
            in_specs=[
                whole(left_factors.shape),
                whole(core.shape),
                pl.BlockSpec(diag_block, lambda i, w, *_: (0, i, 1 - w[0], 0, 0)),
            ],
            out_specs=[whole(mixed_shape), out_spec],
        ),
        out_shape=[
            jax.ShapeDtypeStruct(mixed_shape, jnp.bfloat16),
            jax.ShapeDtypeStruct((tile_count, half, row_dev), jnp.bfloat16),
        ],
        cost_estimate=pl.CostEstimate(flops=flops, bytes_accessed=4 << 20, transcendentals=0),
        compiler_params=pltpu.CompilerParams(vmem_limit_bytes=VMEM_BYTES),
        name="give",
    )(where, tile_ranks, diag_ranks, left_factors, core, diag_rows)
    got = lax.ppermute(given, "panel", swap)
    kept = pl.pallas_call(
        keep_kernel,
        grid_spec=pltpu.PrefetchScalarGridSpec(
            num_scalar_prefetch=1,
            grid=grid,
            in_specs=[
                whole(mixed_shape),
                pl.BlockSpec(diag_block, lambda i, w, *_: (0, i, w[0], 0, 0)),
            ],
            out_specs=out_spec,
        ),
        out_shape=jax.ShapeDtypeStruct((tile_count, half, row_dev), jnp.float32),
        cost_estimate=pl.CostEstimate(flops=flops, bytes_accessed=4 << 20, transcendentals=0),
        compiler_params=pltpu.CompilerParams(vmem_limit_bytes=VMEM_BYTES),
        name="keep",
    )(where, mixed, diag_rows)
    terms = (kept + got.astype(jnp.float32)).astype(jnp.bfloat16)
    parts = lax.all_to_all(
        terms, "panel", split_axis=0, concat_axis=0, tiled=True, axis_index_groups=across
    )
    delta = jnp.sum(parts.astype(jnp.float32), axis=0)
    return target - delta.T


def solution(mesh):
    placed = (
        P("tile", "panel"),
        P("panel", "tile", None),
        P("panel", None, "tile", None),
        P("panel", "tile", None),
        P("panel", "tile", None),
        P("panel", None),
        P("panel"),
    )
    return jax.shard_map(
        shards, mesh=mesh, in_specs=placed, out_specs=P("tile", "panel"), check_vma=False
    )
```

time: 148 us -> 143 us (0.966)
  starting transfers between devices: 20 us -> 12 us
  blocking collectives: 99.9 us -> 106 us
  matrix products: 6.94 us -> 1.75 us
  Pallas kernels: 0 us -> 4.16 us
  waiting for transfers between devices: 2.83 us -> 1.14 us
    ppermute x1 -> x0, starting transfers between devices: 11.3 us -> none  [shards(): both = jnp.concatenate([mixed, lax.ppermute(mixed, 'panel', swap)], 0)]
    psum x1, blocking collectives: 77.8 us -> 83.6 us  [shards(): lax.psum((partial_product * CORE_SCALE).astype(jnp.float16), 'tile')]
    dot_general x2 -> x0, matrix products: 5.4 us -> none  [the longest x1 3.69 us: shards(): jnp.einsum('jcs,jns->cn', diag_rows, both, preferred_element_type=jnp.flo...]
    pallas_call x0 -> x2, Pallas kernels: none -> 4.16 us  [the longest x1 2.33 us: shards(): pl.pallas_call(give_kernel, grid_spec=pltpu.PrefetchScalarGridSpec(num_sc...]
    ppermute x1, starting transfers between devices: 8.79 us -> 12 us  [shards(): got = lax.ppermute(given, 'panel', swap)]
    unnamed x6 -> x14, local copies, waits for them, and re-layouts: 0.02 us -> 2.01 us
    dynamic_slice x2 -> x0, local copies, waits for them, and re-layouts: 1.9 us -> none  [the longest x1 1.03 us: shards(): kept = lax.dynamic_slice_in_dim(diag_left, core_id * half, half, 1)]
    ppermute x1 -> x0, waiting for transfers between devices: 1.89 us -> none  [shards(): both = jnp.concatenate([mixed, lax.ppermute(mixed, 'panel', swap)], 0)]
  transfers between devices with their start and end apart: 3 -> 2, of which waited for: 2 -> 1; matrix products, arithmetic and copies ran while one was open for 3% -> 2% of each run, Pallas kernels for 0% -> 1%
where the time goes in v2:
time: 143 us
  blocking collectives  106 us (74%)
  between operations  13.6 us (10%)
  starting transfers between devices  12 us (8%)
  Pallas kernels  4.16 us (3%)
  other arithmetic  2.32 us (2%)
  local copies, waits for them, and re-layouts  2.01 us (1%)
  matrix products  1.75 us (1%)
    psum x1, blocking collectives, shards(): lax.psum((partial_product * CORE_SCALE).astype(jnp.float16), 'tile')  83.6 us
    all_to_all x1, blocking collectives, shards(): lax.all_to_all(terms, 'panel', split_axis=0, concat_axis=0, tiled=True, a...  22.5 us
    ppermute x1, starting transfers between devices, shards(): got = lax.ppermute(given, 'panel', swap)  12 us
  transfers between devices with their start and end apart: 2, of which 1 were waited for; matrix products, arithmetic and copies ran while one was open for 2% of the time, Pallas kernels for 1%

profile of v2, /device:TPU:1, one launch (start us, length us, event | category | flops | bytes accessed | tf_op | source)
XLA Modules:
  0.0 143.1 jit_solution(2865624407841463929)
XLA Ops:
  6.5 0.0 copy-start
  6.5 0.0 all-gather.2.cloned.1.call-start
  6.5 0.7 all-gather.2.cloned.1.call-update
  7.3 0.1 pad_add_fusion.where
  7.4 0.1 copy-done
  7.5 1.8 %multiply_convert_fusion = f16[3,4,256,256]{3,2,0,1:T(8,128)(2,1)S(1)} fusion(bf16[3,4,128,256]{3,2,1,0:T(8,128)(2,1)} %param.9, bf16[3,128,256]{2,1,0:T(8,128)(2,1)S(1)} %copy-done), kind=kOutput, calls=%fused_computation | convolution fusion | flops 202899456 | bytes 2555904 | tf_op jit(solution)/shard_map/jmcr,jcs->jmrs/dot_general | solution.py:71
  9.2 0.0 copy-start.3
  9.2 0.0 copy-start.4
  9.2 0.0 copy-start.5
  9.3 83.6 %all-reduce.1 = u32[3,4,4,8192]{3,2,0,1:T(4,128)} all-reduce(u32[3,4,4,8192]{3,2,0,1:T(4,128)S(1)} %bitcast.14), channel_id=1, replica_groups=mesh['panel'=32,'tile'=16] {'tile'}, use_global_device_ids=true, to_apply=%region_0.1.clone | all-reduce | flops 393216 | bytes 3145728 | tf_op jit(solution)/shard_map/psum | solution.py:74
  92.9 1.1 fusion.1.core
  94.0 0.0 all-gather.2.cloned.1.call-done
  94.0 0.0 copy-done.3
  94.0 1.9 %copy-done.1 = bf16[3,2048,256]{2,1,0:T(8,128)(2,1)S(1)} copy-done((bf16[3,2048,256]{2,1,0:T(8,128)(2,1)S(1)}, bf16[3,2048,256]{2,1,0:T(8,128)(2,1)}, u32[]{:S(2)}) %copy-start.1) | copy-done | bytes 3145752
  95.9 2.3 %give.1 = (bf16[3,256,512]{2,1,0:T(8,128)(2,1)S(1)}, bf16[16,64,512]{2,1,0:T(8,128)(2,1)S(1)}) custom-call(s32[2]{0:T(128)S(1)} %pad_add_fusion.where, s32[3,4]{1,0:T(4,128)S(1)} %copy-done.4, s32[3]{0:T(128)S(1)} %copy-done.5, bf16[3,512,256]{2,1,0:T(8,128)(2,1)S(1)} %copy-done.3, bf16[3,256,256]{2,1,0:T(8,128)(2,1)S(1)} %fusion.1.core, ...), custom_call_target="tpu_custom_call" | custom-call | flops 805306368 | bytes 4194304 | tf_op jit(solution)/shard_map/give/pallas_call | solution.py:85
  98.2 12.0 %collective-permute-start = (bf16[16,64,512]{2,1,0:T(8,128)(2,1)S(1)}, bf16[16,64,512]{2,1,0:T(8,128)(2,1)S(1)}, u32[]{:S(2)}, u32[]{:S(2)}) collective-permute-start(bf16[16,64,512]{2,1,0:T(8,128)(2,1)S(1)} %get-tuple-element.8), channel_id=1, source_target_pairs={{0,16},{16,0},{32,48},{48,32},{64,80},{80,64},{96,112},{112,96},{1... | collective-permute-start | bytes 3145736 | tf_op jit(solution)/shard_map/ppermute | solution.py:105
  110.2 0.0 copy-done.2
  110.2 1.8 %keep.1 = f32[16,64,512]{2,1,0:T(8,128)S(1)} custom-call(s32[2]{0:T(128)S(1)} %pad_add_fusion.where, bf16[3,256,512]{2,1,0:T(8,128)(2,1)S(1)} %get-tuple-element.7.mixed, bf16[3,16,2,64,256]{4,3,2,1,0:T(8,128)(2,1)S(1)} %bitcast.13), custom_call_target="tpu_custom_call" | custom-call | flops 805306368 | bytes 4194304 | tf_op jit(solution)/shard_map/keep/pallas_call | solution.py:106
  112.1 0.4 collective-permute-done
  112.5 0.4 add_convert_fusion
  112.9 0.0 copy-start.6
  112.9 22.5 %all_to_all.5 = bf16[16,64,512]{2,1,0:T(8,128)(2,1)S(1)} all-to-all(bf16[16,64,512]{2,1,0:T(8,128)(2,1)S(1)} %add_convert_fusion), channel_id=1, replica_groups={{0,32,64,96,128,160,192,224,256,288,320,352,384,416,448,480},{16,48,80,..., dimensions={0} | all-to-all | bytes 2097152 | tf_op jit(solution)/shard_map/all_to_all | solution.py:123
  135.4 0.1 convert_reduce_fusion
  135.5 0.7 bitcast_subtract_fusion
  (5 shorter events, 0.0 us)
Async XLA Ops:
  6.5 0.9 copy-start
  6.5 87.4 %all-gather.2.cloned.1.call-start = ((), (), s32[]{:S(2)}) async-start(), calls=%async_computation.1 | async-start | bytes 3342336 | tf_op jit(solution)/shard_map/all_gather | solution.py:68
  9.2 84.8 %copy-start.3 = (bf16[3,512,256]{2,1,0:T(8,128)(2,1)S(1)}, bf16[3,512,256]{2,1,0:T(8,128)(2,1)}, u32[]{:S(2)}) copy-start(bf16[3,512,256]{2,1,0:T(8,128)(2,1)} %left.1) | copy-start | bytes 2359300
  9.2 84.8 %copy-start.4 = (s32[3,4]{1,0:T(4,128)S(1)}, s32[3,4]{1,0:T(4,128)}, u32[]{:S(2)}) copy-start(s32[3,4]{1,0:T(4,128)} %tranks.1) | copy-start | bytes 148
  9.2 84.8 %copy-start.5 = (s32[3]{0:T(128)S(1)}, s32[3]{0:T(128)}, u32[]{:S(2)}) copy-start(s32[3]{0:T(128)} %dranks.1) | copy-start | bytes 40
  94.0 1.9 %copy-start.1 = (bf16[3,2048,256]{2,1,0:T(8,128)(2,1)S(1)}, bf16[3,2048,256]{2,1,0:T(8,128)(2,1)}, u32[]{:S(2)}) copy-start(bf16[3,2048,256]{2,1,0:T(8,128)(2,1)} %all-gather.2.cloned.1.call-done) | copy-start | bytes 9437188
  95.9 14.3 %copy-start.2 = (bf16[3,2048,256]{2,1,0:T(8,128)(2,1)S(1)}, bf16[3,2048,256]{2,1,0:T(8,128)(2,1)}, u32[]{:S(2)}) copy-start(bf16[3,2048,256]{2,1,0:T(8,128)(2,1)} %all-gather.2.cloned.1.call-done) | copy-start | bytes 9437188
  98.2 14.3 %collective-permute-start = (bf16[16,64,512]{2,1,0:T(8,128)(2,1)S(1)}, bf16[16,64,512]{2,1,0:T(8,128)(2,1)S(1)}, u32[]{:S(2)}, u32[]{:S(2)}) collective-permute-start(bf16[16,64,512]{2,1,0:T(8,128)(2,1)S(1)} %get-tuple-element.8), channel_id=1, source_target_pairs={{0,16},{16,0},{32,48},{48,32},{64,80},{80,64},{96,112},{112,96},{1... | collective-permute-start | bytes 3145736 | tf_op jit(solution)/shard_map/ppermute | solution.py:105
  112.9 22.7 %copy-start.6 = (f32[512,64]{0,1:T(8,128)S(1)}, f32[512,64]{0,1:T(8,128)}, u32[]{:S(2)}) copy-start(f32[512,64]{0,1:T(8,128)} %param.7) | copy-start | bytes 393220
Sparse Core Ops, SparseCore 0:
  9.4 83.6 all-gather.1

commit v3 on v1

v3 whole, which is shorter than its diff:
```python
import jax
import jax.numpy as jnp
from jax import lax
from jax.experimental import pallas as pl
from jax.experimental.pallas import tpu as pltpu
from jax.sharding import PartitionSpec as P

CORES = 2
CORE_SCALE = 1024.0
GROUP = 4
VMEM_BYTES = 16 << 20


def mix(where, tranks, dranks, left, core, mixed):
    columns, _, rank = left.shape
    row = lax.broadcasted_iota(jnp.int32, (rank, rank), 0)
    col = lax.broadcasted_iota(jnp.int32, (rank, rank), 1)
    for j in range(columns):
        keep = (row < tranks[j, where[1]]) & (col < dranks[j])
        masked = jnp.where(keep, core[j].astype(jnp.float32), 0.0).astype(jnp.bfloat16)
        mixed[j] = lax.dot_general(
            masked, left[j], (((0,), (1,)), ((), ())), preferred_element_type=jnp.float32
        ).astype(jnp.bfloat16)


def expand(first, diag, mixed, out):
    columns, _, half, rank = diag.shape
    total = None
    for j in range(columns):
        block = diag[j, first : first + GROUP].reshape(GROUP * half, rank)
        part = jnp.dot(block, mixed[j], preferred_element_type=jnp.float32)
        total = part if total is None else total + part
    out[first : first + GROUP] = total.reshape(GROUP, half, -1).astype(out.dtype)


def give_kernel(where, tranks, dranks, left, core, diag, mixed, given, diag_kept, held, arrived, kept):
    tiles = held.shape[1]
    groups = range(0, tiles, GROUP)

    def fetch(n, first):
        part = pl.ds(first, GROUP)
        return pltpu.make_async_copy(
            diag.at[:, part, 1 - where[0]], held.at[:, part], arrived.at[n]
        )

    rest = pltpu.make_async_copy(diag.at[:, :, where[0]], diag_kept, kept)
    for n, first in enumerate(groups):
        fetch(n, first).start()
    rest.start()
    mix(where, tranks, dranks, left, core, mixed)
    for n, first in enumerate(groups):
        fetch(n, first).wait()
        expand(first, held, mixed, given)
    rest.wait()


def keep_kernel(mixed, diag, out):
    for first in range(0, diag.shape[1], GROUP):
        expand(first, diag, mixed, out)


def shards(target, left_factors, right_factors, diag_left, diag_right, tile_ranks, diag_ranks):
    column_count, row_dev, rank = left_factors.shape
    piece = diag_left.shape[1]
    tile_count = lax.axis_size("tile")
    panel_count = lax.axis_size("panel")
    chip_count = panel_count // CORES
    half = piece // CORES
    tile_size = piece * tile_count
    local_tile = lax.axis_index("tile") * row_dev // tile_size
    core_id = lax.axis_index("panel") % CORES
    swap = [(p, p ^ 1) for p in range(panel_count)]
    across = [[CORES * c + a for c in range(chip_count)] for a in range(CORES)]

    diag_rows = lax.all_gather(diag_left, "tile", axis=1, tiled=True)
    diag_rows = diag_rows.reshape(column_count, tile_count, CORES, half, rank)
    diag_rows = pltpu.with_memory_space_constraint(diag_rows, pltpu.HBM)

    partial_product = jnp.einsum(
        "jmcr,jcs->jmrs", right_factors, diag_right, preferred_element_type=jnp.float32
    )
    core_sum = lax.psum((partial_product * CORE_SCALE).astype(jnp.float16), "tile")
    mine = lax.dynamic_index_in_dim(core_sum, local_tile, 1, keepdims=False)
    core = (mine.astype(jnp.float32) * (1.0 / CORE_SCALE)).astype(jnp.bfloat16)

    where = jnp.stack([core_id, local_tile]).astype(jnp.int32)
    flops = 2 * column_count * tile_count * half * rank * row_dev
    cost = pl.CostEstimate(flops=flops, bytes_accessed=4 << 20, transcendentals=0)
    params = pltpu.CompilerParams(vmem_limit_bytes=VMEM_BYTES)
    smem = pl.BlockSpec(memory_space=pltpu.SMEM)
    vmem = pl.BlockSpec(memory_space=pltpu.VMEM)
    diag_half = (column_count, tile_count, half, rank)
    product = (tile_count, half, row_dev)

    mixed, given, diag_kept = pl.pallas_call(
        give_kernel,
        in_specs=[smem, smem, smem, vmem, vmem, pl.BlockSpec(memory_space=pltpu.HBM)],
        out_specs=[vmem, vmem, vmem],
        out_shape=[
            jax.ShapeDtypeStruct((column_count, rank, row_dev), jnp.bfloat16),
            jax.ShapeDtypeStruct(product, jnp.bfloat16),
            jax.ShapeDtypeStruct(diag_half, jnp.bfloat16),
        ],
        scratch_shapes=[
            pltpu.VMEM(diag_half, jnp.bfloat16),
            pltpu.SemaphoreType.DMA((tile_count // GROUP,)),
            pltpu.SemaphoreType.DMA,
        ],
        cost_estimate=cost,
        compiler_params=params,
        name="give",
    )(where, tile_ranks, diag_ranks, left_factors, core, diag_rows)
    got = lax.ppermute(given, "panel", swap)
    kept = pl.pallas_call(
        keep_kernel,
        in_specs=[vmem, vmem],
        out_specs=vmem,
        out_shape=jax.ShapeDtypeStruct(product, jnp.float32),
        cost_estimate=cost,
        compiler_params=params,
        name="keep",
    )(mixed, diag_kept)
    terms = (kept + got.astype(jnp.float32)).astype(jnp.bfloat16)
    parts = lax.all_to_all(
        terms, "panel", split_axis=0, concat_axis=0, tiled=True, axis_index_groups=across
    )
    delta = jnp.sum(parts.astype(jnp.float32), axis=0)
    return target - delta.T


def solution(mesh):
    placed = (
        P("tile", "panel"),
        P("panel", "tile", None),
        P("panel", None, "tile", None),
        P("panel", "tile", None),
        P("panel", "tile", None),
        P("panel", None),
        P("panel"),
    )
    return jax.shard_map(
        shards, mesh=mesh, in_specs=placed, out_specs=P("tile", "panel"), check_vma=False
    )
```

time: 148 us -> 142 us (0.959)
  starting transfers between devices: 20 us -> 12 us
  blocking collectives: 99.9 us -> 106 us
  matrix products: 6.94 us -> 1.75 us
  Pallas kernels: 0 us -> 4.08 us
  local copies, waits for them, and re-layouts: 1.91 us -> 0.13 us
    ppermute x1 -> x0, starting transfers between devices: 11.3 us -> none  [shards(): both = jnp.concatenate([mixed, lax.ppermute(mixed, 'panel', swap)], 0)]
    psum x1, blocking collectives: 77.8 us -> 83.6 us  [shards(): lax.psum((partial_product * CORE_SCALE).astype(jnp.float16), 'tile')]
    dot_general x2 -> x0, matrix products: 5.4 us -> none  [the longest x1 3.69 us: shards(): jnp.einsum('jcs,jns->cn', diag_rows, both, preferred_element_type=jnp.flo...]
    pallas_call x0 -> x2, Pallas kernels: none -> 4.08 us  [the longest x1 3.11 us: shards(): pl.pallas_call(give_kernel, in_specs=[smem, smem, smem, vmem, vmem, pl.Bl...]
    ppermute x1, starting transfers between devices: 8.79 us -> 12 us  [shards(): got = lax.ppermute(given, 'panel', swap)]
    dynamic_slice x2 -> x0, local copies, waits for them, and re-layouts: 1.9 us -> none  [the longest x1 1.03 us: shards(): kept = lax.dynamic_slice_in_dim(diag_left, core_id * half, half, 1)]
    ppermute x1 -> x0, waiting for transfers between devices: 1.89 us -> none  [shards(): both = jnp.concatenate([mixed, lax.ppermute(mixed, 'panel', swap)], 0)]
  transfers between devices with their start and end apart: 3 -> 2, of which waited for: 2 -> 1; matrix products, arithmetic and copies ran while one was open for 3% -> 2% of each run, Pallas kernels for 0% -> 1%
where the time goes in v3:
time: 142 us
  blocking collectives  106 us (75%)
  between operations  13.5 us (10%)
  starting transfers between devices  12 us (8%)
  Pallas kernels  4.08 us (3%)
  other arithmetic  2.34 us (2%)
  waiting for transfers between devices  2.02 us (1%)
  matrix products  1.75 us (1%)
    psum x1, blocking collectives, shards(): lax.psum((partial_product * CORE_SCALE).astype(jnp.float16), 'tile')  83.6 us
    all_to_all x1, blocking collectives, shards(): lax.all_to_all(terms, 'panel', split_axis=0, concat_axis=0, tiled=True, a...  22.5 us
    ppermute x1, starting transfers between devices, shards(): got = lax.ppermute(given, 'panel', swap)  12 us
    pallas_call x1, Pallas kernels, shards(): pl.pallas_call(give_kernel, in_specs=[smem, smem, smem, vmem, vmem, pl.Bl...  3.11 us
  transfers between devices with their start and end apart: 2, of which 1 were waited for; matrix products, arithmetic and copies ran while one was open for 2% of the time, Pallas kernels for 1%

profile of v3, /device:TPU:1, one launch (start us, length us, event | category | flops | bytes accessed | tf_op | source)
XLA Modules:
  0.0 142.0 jit_solution(17530931550168509104)
XLA Ops:
  6.5 0.0 copy-start
  6.5 0.0 all-gather.2.cloned.1.call-start
  6.5 0.7 all-gather.2.cloned.1.call-update
  7.3 0.1 pad_add_fusion.where
  7.4 0.1 copy-done
  7.5 1.8 %multiply_convert_fusion = f16[3,4,256,256]{3,2,0,1:T(8,128)(2,1)S(1)} fusion(bf16[3,4,128,256]{3,2,1,0:T(8,128)(2,1)} %param.9, bf16[3,128,256]{2,1,0:T(8,128)(2,1)S(1)} %copy-done), kind=kOutput, calls=%fused_computation | convolution fusion | flops 202899456 | bytes 2555904 | tf_op jit(solution)/shard_map/jmcr,jcs->jmrs/dot_general | solution.py:79
  9.2 0.0 copy-start.1
  9.2 0.0 copy-start.2
  9.2 0.0 copy-start.3
  9.3 83.6 %all-reduce.1 = u32[3,4,4,8192]{3,2,0,1:T(4,128)} all-reduce(u32[3,4,4,8192]{3,2,0,1:T(4,128)S(1)} %bitcast.12), channel_id=1, replica_groups=mesh['panel'=32,'tile'=16] {'tile'}, use_global_device_ids=true, to_apply=%region_0.1.clone | all-reduce | flops 393216 | bytes 3145728 | tf_op jit(solution)/shard_map/psum | solution.py:82
  92.9 1.1 fusion.1.core
  94.0 0.0 all-gather.2.cloned.1.call-done
  94.0 0.0 copy-done.1
  94.0 0.0 copy-done.2
  94.0 3.1 %give.1 = (bf16[3,256,512]{2,1,0:T(8,128)(2,1)S(1)}, bf16[16,64,512]{2,1,0:T(8,128)(2,1)S(1)}, bf16[3,16,64,256]{3,2,1,0:T(8,128)(2,1)S(1)}) custom-call(s32[2]{0:T(128)S(1)} %pad_add_fusion.where, s32[3,4]{1,0:T(4,128)S(1)} %copy-done.2, s32[3]{0:T(128)S(1)} %copy-done.3, bf16[3,512,256]{2,1,0:T(8,128)(2,1)S(1)} %copy-done.1, ...), custom_call_target="tpu_custom_call" | custom-call | flops 805306368 | bytes 4194304 | tf_op jit(solution)/shard_map/give/pallas_call | solution.py:95
  97.1 12.0 %collective-permute-start = (bf16[16,64,512]{2,1,0:T(8,128)(2,1)S(1)}, bf16[16,64,512]{2,1,0:T(8,128)(2,1)S(1)}, u32[]{:S(2)}, u32[]{:S(2)}) collective-permute-start(bf16[16,64,512]{2,1,0:T(8,128)(2,1)S(1)} %get-tuple-element.10), channel_id=1, source_target_pairs={{0,16},{16,0},{32,48},{48,32},{64,80},{80,64},{96,112},{112,96},{1... | collective-permute-start | bytes 3145736 | tf_op jit(solution)/shard_map/ppermute | solution.py:113
  109.1 1.0 keep.1
  110.1 1.3 collective-permute-done
  111.4 0.4 add_convert_fusion
  111.8 0.0 copy-start.4
  111.8 22.5 %all_to_all.5 = bf16[16,64,512]{2,1,0:T(8,128)(2,1)S(1)} all-to-all(bf16[16,64,512]{2,1,0:T(8,128)(2,1)S(1)} %add_convert_fusion), channel_id=1, replica_groups={{0,32,64,96,128,160,192,224,256,288,320,352,384,416,448,480},{16,48,80,..., dimensions={0} | all-to-all | bytes 2097152 | tf_op jit(solution)/shard_map/all_to_all | solution.py:124
  134.3 0.1 convert_reduce_fusion
  134.4 0.0 copy-done.4
  134.4 0.7 bitcast_subtract_fusion
  (1 shorter events, 0.0 us)
Async XLA Ops:
  6.5 0.9 copy-start
  6.5 87.4 %all-gather.2.cloned.1.call-start = ((), (), s32[]{:S(2)}) async-start(), calls=%async_computation.1 | async-start | bytes 3342336 | tf_op jit(solution)/shard_map/all_gather | solution.py:75
  9.2 84.8 %copy-start.1 = (bf16[3,512,256]{2,1,0:T(8,128)(2,1)S(1)}, bf16[3,512,256]{2,1,0:T(8,128)(2,1)}, u32[]{:S(2)}) copy-start(bf16[3,512,256]{2,1,0:T(8,128)(2,1)} %left.1) | copy-start | bytes 2359300
  9.2 84.8 %copy-start.2 = (s32[3,4]{1,0:T(4,128)S(1)}, s32[3,4]{1,0:T(4,128)}, u32[]{:S(2)}) copy-start(s32[3,4]{1,0:T(4,128)} %tranks.1) | copy-start | bytes 148
  9.2 84.8 %copy-start.3 = (s32[3]{0:T(128)S(1)}, s32[3]{0:T(128)}, u32[]{:S(2)}) copy-start(s32[3]{0:T(128)} %dranks.1) | copy-start | bytes 40
  97.1 14.3 %collective-permute-start = (bf16[16,64,512]{2,1,0:T(8,128)(2,1)S(1)}, bf16[16,64,512]{2,1,0:T(8,128)(2,1)S(1)}, u32[]{:S(2)}, u32[]{:S(2)}) collective-permute-start(bf16[16,64,512]{2,1,0:T(8,128)(2,1)S(1)} %get-tuple-element.10), channel_id=1, source_target_pairs={{0,16},{16,0},{32,48},{48,32},{64,80},{80,64},{96,112},{112,96},{1... | collective-permute-start | bytes 3145736 | tf_op jit(solution)/shard_map/ppermute | solution.py:113
  111.8 22.7 %copy-start.4 = (f32[512,64]{0,1:T(8,128)S(1)}, f32[512,64]{0,1:T(8,128)}, u32[]{:S(2)}) copy-start(f32[512,64]{0,1:T(8,128)} %param.7) | copy-start | bytes 393220
Sparse Core Ops, SparseCore 0:
  9.4 83.6 all-gather.1

commit v4 on v1

v4 whole, which is shorter than its diff:
```python
import jax
import jax.numpy as jnp
from jax import lax
from jax.sharding import PartitionSpec as P

CORES = 2
CORE_SCALE = 2.0**10
DIAG_SCALE = 2.0**15


def shards(target, left_factors, right_factors, diag_left, diag_right, tile_ranks, diag_ranks):
    column_count, row_dev, rank = left_factors.shape
    tiles = right_factors.shape[1]
    piece = diag_left.shape[1]
    tile_count = lax.axis_size("tile")
    panel_count = lax.axis_size("panel")
    chip_count = panel_count // CORES
    half = piece // CORES
    columns = CORES * column_count
    tile_size = piece * tile_count
    local_tile = lax.axis_index("tile") * row_dev // tile_size
    first_core = lax.axis_index("panel") % CORES == 0
    swap = [(p, p ^ 1) for p in range(panel_count)]
    to_second = [(CORES * c, CORES * c + 1) for c in range(chip_count)]
    to_first = [(CORES * c + 1, CORES * c) for c in range(chip_count)]
    across = [[CORES * c + a for c in range(chip_count)] for a in range(CORES)]

    positions = jnp.arange(rank)
    right = jnp.where(positions < tile_ranks[:, :, None, None], right_factors, 0)
    diag = jnp.where(positions < diag_ranks[:, None, None], diag_right, 0)

    small = lax.ppermute(jnp.where(first_core, diag, diag_left), "panel", swap)
    large = lax.ppermute(
        jnp.where(first_core, right.reshape(left_factors.shape), left_factors), "panel", swap
    )

    def gather(right, diag, diag_left, small, large):
        both = jnp.concatenate([small, diag_left], 0).reshape(columns, CORES, half, rank)
        both = both.transpose(1, 2, 0, 3).reshape(CORES, half, columns * rank)
        both = (both.astype(jnp.float32) * DIAG_SCALE).astype(jnp.float16)
        rows = lax.all_gather(both, "tile", axis=1, tiled=True)
        return rows, jnp.zeros((columns, rank, rank), jnp.bfloat16)

    def reduce(right, diag, diag_left, small, large):
        right = jnp.concatenate([right, large.reshape(right.shape)], 0)
        diag = jnp.concatenate([diag, small], 0)
        partial_product = jnp.einsum(
            "jmcr,jcs->mjrs", right, diag, preferred_element_type=jnp.float32
        )
        total = lax.psum((partial_product * CORE_SCALE).astype(jnp.float16), "tile")
        mine = lax.dynamic_index_in_dim(total, local_tile, 0, keepdims=False)
        core = (mine.astype(jnp.float32) * (1.0 / CORE_SCALE)).astype(jnp.bfloat16)
        return jnp.zeros((CORES, half * tile_count, columns * rank), jnp.float16), core

    rows, core = lax.cond(
        first_core, gather, reduce, right, diag, diag_left, small, large
    )
    core = lax.ppermute(core, "panel", to_first)
    left = jnp.concatenate([large, left_factors], 0)
    mixed = jnp.einsum("jrs,jnr->jsn", core, left, preferred_element_type=jnp.float32)
    mixed = mixed.astype(jnp.bfloat16).reshape(columns * rank, row_dev)

    def expand(a):
        out = jnp.dot(rows[a].astype(jnp.bfloat16), mixed, preferred_element_type=jnp.float32)
        out = (out * (1.0 / DIAG_SCALE)).astype(jnp.bfloat16)
        return out.reshape(tile_count, half, row_dev)

    got = lax.ppermute(expand(1), "panel", to_second)
    terms = jnp.where(first_core, expand(0), got)
    parts = lax.all_to_all(
        terms, "panel", split_axis=0, concat_axis=0, tiled=True, axis_index_groups=across
    )
    delta = jnp.sum(parts.astype(jnp.float32), axis=0)
    return target - delta.T


def solution(mesh):
    placed = (
        P("tile", "panel"),
        P("panel", "tile", None),
        P("panel", None, "tile", None),
        P("panel", "tile", None),
        P("panel", "tile", None),
        P("panel", None),
        P("panel"),
    )
    return jax.shard_map(
        shards, mesh=mesh, in_specs=placed, out_specs=P("tile", "panel"), check_vma=False
    )
```

time: 148 us -> 136 us (0.919)
  between operations: 13.5 us -> 0.15 us
  blocking collectives: 99.9 us -> 94.9 us
  matrix products: 6.94 us -> 9.32 us
  waiting for transfers between devices: 2.83 us -> 4.8 us
  starting transfers between devices: 20 us -> 21.9 us
    psum x1, blocking collectives: 77.8 us -> 72.4 us  [reduce(): total = lax.psum((partial_product * CORE_SCALE).astype(jnp.float16), 'tile')]
    dot_general x3 -> x4, matrix products: 6.94 us -> 9.32 us  [the longest x1 3.77 us: reduce(): jnp.einsum('jmcr,jcs->mjrs', right, diag, preferred_element_type=jnp.floa...]
    ppermute x2 -> x4, waiting for transfers between devices: 2.81 us -> 4.8 us  [the longest x1 1.84 us: shards(): core = lax.ppermute(core, 'panel', to_first)]
    ppermute x2 -> x4, starting transfers between devices: 20 us -> 21.9 us  [the longest x1 9.96 us: shards(): core = lax.ppermute(core, 'panel', to_first)]
    dynamic_slice x2 -> x0, local copies, waits for them, and re-layouts: 1.9 us -> none  [the longest x1 1.03 us: shards(): kept = lax.dynamic_slice_in_dim(diag_left, core_id * half, half, 1)]
    select_n x0 -> x4, other arithmetic: none -> 1.8 us  [the longest x1 1.2 us: shards(): jnp.where(positions < tile_ranks[:, :, None, None], right_factors, 0)]
  transfers between devices with their start and end apart: 3 -> 4, of which waited for: 2 -> 3; matrix products, arithmetic and copies ran while one was open for 3% -> 2% of each run, Pallas kernels for 0% -> 0%
where the time goes in v4:
time: 136 us
  blocking collectives  94.9 us (70%)
  starting transfers between devices  21.9 us (16%)
  matrix products  9.32 us (7%)
  waiting for transfers between devices  4.8 us (4%)
  other arithmetic  3.71 us (3%)
    psum x1, blocking collectives, reduce(): total = lax.psum((partial_product * CORE_SCALE).astype(jnp.float16), 'tile')  72.4 us
    all_to_all x1, blocking collectives, shards(): lax.all_to_all(terms, 'panel', split_axis=0, concat_axis=0, tiled=True, a...  22.5 us
    ppermute x1, starting transfers between devices, shards(): core = lax.ppermute(core, 'panel', to_first)  9.96 us
    ppermute x1, starting transfers between devices, shards(): lax.ppermute(jnp.where(first_core, right.reshape(left_factors.shape), lef...  8.77 us
    dot_general x1, matrix products, reduce(): jnp.einsum('jmcr,jcs->mjrs', right, diag, preferred_element_type=jnp.floa...  3.77 us
    dot_general x2, matrix products, expand(): jnp.dot(rows[a].astype(jnp.bfloat16), mixed, preferred_element_type=jnp.f...  3.57 us
  transfers between devices with their start and end apart: 4, of which 3 were waited for; matrix products, arithmetic and copies ran while one was open for 2% of the time, Pallas kernels for 0%

profile of v4, /device:TPU:1, one launch (start us, length us, event | category | flops | bytes accessed | tf_op | source)
XLA Modules:
  0.0 135.7 jit_solution(16004253884117118808)
XLA Ops:
  0.0 0.8 iota_compare_fusion
  0.9 1.2 broadcast_select_fusion.1
  2.1 0.1 bitcast_select_fusion
  2.2 8.8 %collective-permute-start.1 = (bf16[3,512,256]{2,1,0:T(8,128)(2,1)S(1)}, bf16[3,512,256]{2,1,0:T(8,128)(2,1)}, u32[]{:S(2)}, u32[]{:S(2)}) collective-permute-start(bf16[3,512,256]{2,1,0:T(8,128)(2,1)S(1)} %bitcast_select_fusion), channel_id=1, source_target_pairs={{0,16},{16,0},{32,48},{48,32},{64,80},{80,64},{96,112},{112,96},{1... | collective-permute-start | bytes 2359304 | tf_op jit(solution)/shard_map/ppermute | solution.py:33
  11.1 0.4 copy_select_fusion
  11.5 1.9 %collective-permute-start = (bf16[3,128,256]{2,0,1:T(4,128)(2,1)S(1)}, bf16[3,128,256]{2,0,1:T(4,128)(2,1)S(1)}, u32[]{:S(2)}, u32[]{:S(2)}) collective-permute-start(bf16[3,128,256]{2,0,1:T(4,128)(2,1)S(1)} %get-tuple-element.82), channel_id=1, source_target_pairs={{0,16},{16,0},{32,48},{48,32},{64,80},{80,64},{96,112},{112,96},{1... | collective-permute-start | bytes 589832 | tf_op jit(solution)/shard_map/ppermute | solution.py:32
  13.4 1.5 %collective-permute-done = bf16[3,128,256]{2,0,1:T(4,128)(2,1)S(1)} collective-permute-done((bf16[3,128,256]{2,0,1:T(4,128)(2,1)S(1)}, bf16[3,128,256]{2,0,1:T(4,128)(2,1)S(1)}, u32[]{:S(2)}, u32[]{:S(2)}) %collective-permute-start) | collective-permute-done | bytes 196640 | tf_op jit(solution)/shard_map/ppermute | solution.py:32
  14.9 77.2 %conditional.1 = (f16[2,1024,1536]{2,1,0:T(8,128)(2,1)S(1)}, bf16[6,256,256]{1,2,0:T(8,128)(2,1)S(1)}) conditional(s32[]{:T(128)} %convert_element_type.60, (bf16[3,128,256]{2,0,1:T(4,128)(2,1)S(1)}, bf16[3,128,256]{2,0,1:T(4,128)(2,1)S(1)}, bf16[3,512,256]{2,1,0:T(8,128)(2,1)}, bf16[3,4,128,256]{3,2,1,0:T(8,128)(2,1)S(1)}, s32[]{:T(128)}, /*index=5*/(), ...), branch_computations={%region_0.2_spmd, %region_2.3_spmd} | conditional | flops 411697152 | bytes 20054228 | solution.py:55
  14.9 0.2 copy.15
  15.1 0.2 copy.16
  15.3 3.8 %multiply_convert_fusion.1 = f16[6,256,4,256]{3,1,2,0:T(8,128)(2,1)} fusion(bf16[3,4,128,256]{3,2,1,0:T(8,128)(2,1)} %bitcast.2, bf16[3,4,128,256]{3,2,1,0:T(8,128)(2,1)S(1)} %get-tuple-element.50, bf16[3,128,256]{1,2,0:T(8,128)(2,1)S(1)} %copy.16, bf16[3,128,256]{1,2,0:T(8,128)(2,1)S(1)} %copy.15), kind=kOutput, calls=%fused_computation.1 | convolution fusion | flops 409731072 | bytes 5111808 | tf_op jit(solution)/shard_map/cond/branch_0_fun/jmcr,jcs->mjrs/dot_general | solution.py:47
  19.1 72.4 %all-reduce.1 = u32[4,6,8192,4]{2,3,0,1:T(4,128)S(1)} all-reduce(u32[4,6,8192,4]{2,3,0,1:T(4,128)} %bitcast.37), channel_id=1, replica_groups=mesh['panel'=32,'tile'=16] {'tile'}, use_global_device_ids=true, to_apply=%region_1.1.clone | all-reduce | flops 786432 | bytes 6291456 | tf_op jit(solution)/shard_map/cond/branch_0_fun/psum | solution.py:50
  91.5 0.2 fusion.3
  91.7 0.4 broadcast.47
  92.1 10.0 %collective-permute-start.2 = (bf16[6,256,256]{1,2,0:T(8,128)(2,1)S(1)}, bf16[6,256,256]{1,2,0:T(8,128)(2,1)S(1)}, u32[]{:S(2)}, u32[]{:S(2)}) collective-permute-start(bf16[6,256,256]{1,2,0:T(8,128)(2,1)S(1)} %get-tuple-element.59), channel_id=1, source_target_pairs={{16,0},{48,32},{80,64},{112,96},{144,128},{176,160},{208,192},{240... | collective-permute-start | bytes 2359304 | tf_op jit(solution)/shard_map/ppermute | solution.py:58
  102.1 1.8 %collective-permute-done.2 = bf16[6,256,256]{1,2,0:T(8,128)(2,1)S(1)} collective-permute-done((bf16[6,256,256]{1,2,0:T(8,128)(2,1)S(1)}, bf16[6,256,256]{1,2,0:T(8,128)(2,1)S(1)}, u32[]{:S(2)}, u32[]{:S(2)}) %collective-permute-start.2) | collective-permute-done | bytes 786464 | tf_op jit(solution)/shard_map/ppermute | solution.py:58
  103.9 2.0 %convolution_convert_fusion = bf16[6,256,512]{2,1,0:T(8,128)(2,1)S(1)} fusion(bf16[6,256,256]{1,2,0:T(8,128)(2,1)S(1)} %collective-permute-done.2, bf16[3,512,256]{2,1,0:T(8,128)(2,1)} %param.10, bf16[3,512,256]{2,1,0:T(8,128)(2,1)} %collective-permute-done.1), kind=kOutput, calls=%fused_computation.22 | convolution fusion | flops 404226048 | bytes 3932160 | tf_op jit(solution)/shard_map/jrs,jnr->jsn/dot_general | solution.py:60
  105.9 1.8 %multiply_convert_fusion.3 = bf16[1024,512]{1,0:T(8,128)(2,1)S(1)} fusion(bf16[1536,512]{1,0:T(8,128)(2,1)S(1)} %bitcast.41, f16[2,1024,1536]{2,1,0:T(8,128)(2,1)S(1)} %get-tuple-element.58), kind=kOutput, calls=%fused_computation.20 | convolution fusion | flops 1613234176 | bytes 5767168 | tf_op jit(solution)/shard_map/dot_general | solution.py:64
  107.7 1.3 collective-permute-start.3
  109.0 1.8 %multiply_convert_fusion.4 = bf16[1024,512]{1,0:T(8,128)(2,1)S(1)} fusion(bf16[1536,512]{1,0:T(8,128)(2,1)S(1)} %bitcast.42, f16[2,1024,1536]{2,1,0:T(8,128)(2,1)S(1)} %get-tuple-element.58), kind=kOutput, calls=%fused_computation.21 | convolution fusion | flops 1613234176 | bytes 5767168 | tf_op jit(solution)/shard_map/dot_general | solution.py:64
  110.8 1.5 %collective-permute-done.3 = bf16[16,64,512]{2,1,0:T(8,128)(2,1)S(1)} collective-permute-done((bf16[16,64,512]{2,1,0:T(8,128)(2,1)S(1)}, bf16[16,64,512]{2,1,0:T(8,128)(2,1)S(1)}, u32[]{:S(2)}, u32[]{:S(2)}) %collective-permute-start.3) | collective-permute-done | bytes 1048608 | tf_op jit(solution)/shard_map/ppermute | solution.py:68
  112.4 22.5 %all_to_all.5 = bf16[16,64,512]{2,1,0:T(8,128)(2,1)S(1)} all-to-all(bf16[16,64,512]{2,1,0:T(8,128)(2,1)S(1)} %broadcast_select_fusion), channel_id=1, replica_groups={{0,32,64,96,128,160,192,224,256,288,320,352,384,416,448,480},{16,48,80,..., dimensions={0} | all-to-all | bytes 2097152 | tf_op jit(solution)/shard_map/all_to_all | solution.py:70
  134.8 0.1 convert_reduce_fusion
  135.0 0.7 bitcast_subtract_fusion
  (13 shorter events, 0.2 us)
Async XLA Ops:
  0.0 2.1 %copy-start = (bf16[3,512,256]{2,1,0:T(8,128)(2,1)S(1)}, bf16[3,512,256]{2,1,0:T(8,128)(2,1)}, u32[]{:S(2)}) copy-start(bf16[3,512,256]{2,1,0:T(8,128)(2,1)} %param.10) | copy-start | bytes 2359300
  0.0 11.0 %copy-start.4 = (s32[3]{0:T(128)S(1)}, s32[3]{0:T(128)}, u32[]{:S(2)}) copy-start(s32[3]{0:T(128)} %param.15) | copy-start | bytes 40
  0.0 11.1 %copy-start.1 = (bf16[3,128,256]{2,1,0:T(8,128)(2,1)S(1)}, bf16[3,128,256]{2,1,0:T(8,128)(2,1)}, u32[]{:S(2)}) copy-start(bf16[3,128,256]{2,1,0:T(8,128)(2,1)} %param.12) | copy-start | bytes 589828
  0.0 11.1 %copy-start.2 = (bf16[3,128,256]{2,1,0:T(8,128)(2,1)S(1)}, bf16[3,128,256]{2,1,0:T(8,128)(2,1)}, u32[]{:S(2)}) copy-start(bf16[3,128,256]{2,1,0:T(8,128)(2,1)} %param.13) | copy-start | bytes 589828
  2.2 12.7 %collective-permute-start.1 = (bf16[3,512,256]{2,1,0:T(8,128)(2,1)S(1)}, bf16[3,512,256]{2,1,0:T(8,128)(2,1)}, u32[]{:S(2)}, u32[]{:S(2)}) collective-permute-start(bf16[3,512,256]{2,1,0:T(8,128)(2,1)S(1)} %bitcast_select_fusion), channel_id=1, source_target_pairs={{0,16},{16,0},{32,48},{48,32},{64,80},{80,64},{96,112},{112,96},{1... | collective-permute-start | bytes 2359304 | tf_op jit(solution)/shard_map/ppermute | solution.py:33
  11.5 3.4 %collective-permute-start = (bf16[3,128,256]{2,0,1:T(4,128)(2,1)S(1)}, bf16[3,128,256]{2,0,1:T(4,128)(2,1)S(1)}, u32[]{:S(2)}, u32[]{:S(2)}) collective-permute-start(bf16[3,128,256]{2,0,1:T(4,128)(2,1)S(1)} %get-tuple-element.82), channel_id=1, source_target_pairs={{0,16},{16,0},{32,48},{48,32},{64,80},{80,64},{96,112},{112,96},{1... | collective-permute-start | bytes 589832 | tf_op jit(solution)/shard_map/ppermute | solution.py:32
  92.1 11.8 %collective-permute-start.2 = (bf16[6,256,256]{1,2,0:T(8,128)(2,1)S(1)}, bf16[6,256,256]{1,2,0:T(8,128)(2,1)S(1)}, u32[]{:S(2)}, u32[]{:S(2)}) collective-permute-start(bf16[6,256,256]{1,2,0:T(8,128)(2,1)S(1)} %get-tuple-element.59), channel_id=1, source_target_pairs={{16,0},{48,32},{80,64},{112,96},{144,128},{176,160},{208,192},{240... | collective-permute-start | bytes 2359304 | tf_op jit(solution)/shard_map/ppermute | solution.py:58
  107.7 4.6 %collective-permute-start.3 = (bf16[16,64,512]{2,1,0:T(8,128)(2,1)S(1)}, bf16[16,64,512]{2,1,0:T(8,128)(2,1)S(1)}, u32[]{:S(2)}, u32[]{:S(2)}) collective-permute-start(bf16[16,64,512]{2,1,0:T(8,128)(2,1)S(1)} %bitcast.40), channel_id=1, source_target_pairs={{0,16},{32,48},{64,80},{96,112},{128,144},{160,176},{192,208},{224... | collective-permute-start | bytes 3145736 | tf_op jit(solution)/shard_map/ppermute | solution.py:68
  112.4 22.6 %copy-start.3 = (f32[512,64]{0,1:T(8,128)S(1)}, f32[512,64]{0,1:T(8,128)}, u32[]{:S(2)}) copy-start(f32[512,64]{0,1:T(8,128)} %param.9) | copy-start | bytes 393220

commit v5 on v4

v5 whole, which is shorter than its diff:
```python
import jax
import jax.numpy as jnp
from jax import lax
from jax.experimental import pallas as pl
from jax.experimental.pallas import tpu as pltpu
from jax.sharding import PartitionSpec as P

CORES = 2
CORE_SCALE = 2.0**10
DIAG_SCALE = 2.0**15
VMEM_BYTES = 12 << 20


def mix_kernel(place, tranks, dranks, bundle, ours, mixed):
    columns, row_dev, rank = ours.shape
    cores = CORES * columns
    blocks = row_dev // rank
    row = lax.broadcasted_iota(jnp.int32, (rank, rank), 0)
    col = lax.broadcasted_iota(jnp.int32, (rank, rank), 1)
    for j in range(cores):
        core = bundle[j]
        if j < columns:
            first = cores + blocks * j
            left = bundle[first : first + blocks].reshape(row_dev, rank)
        else:
            mine = j - columns
            keep = (col < tranks[mine, place[0]]) & (row < dranks[mine])
            core = jnp.where(keep, core.astype(jnp.float32), 0.0).astype(core.dtype)
            left = ours[mine]
        part = lax.dot_general(
            core, left, (((1,), (1,)), ((), ())), preferred_element_type=jnp.float32
        )
        mixed[j * rank : (j + 1) * rank] = part.astype(mixed.dtype)


def shards(target, left_factors, right_factors, diag_left, diag_right, tile_ranks, diag_ranks):
    column_count, row_dev, rank = left_factors.shape
    piece = diag_left.shape[1]
    tile_count = lax.axis_size("tile")
    panel_count = lax.axis_size("panel")
    chip_count = panel_count // CORES
    half = piece // CORES
    columns = CORES * column_count
    tile_size = piece * tile_count
    local_tile = lax.axis_index("tile") * row_dev // tile_size
    gathers = lax.axis_index("panel") % CORES == 0
    swap = [(p, p ^ 1) for p in range(panel_count)]
    to_second = [(CORES * c, CORES * c + 1) for c in range(chip_count)]
    to_first = [(CORES * c + 1, CORES * c) for c in range(chip_count)]
    across = [[CORES * c + a for c in range(chip_count)] for a in range(CORES)]

    small = lax.ppermute(jnp.where(gathers, diag_right, diag_left), "panel", swap)
    their_right = lax.ppermute(right_factors, "panel", to_second)

    both = jnp.concatenate([small, diag_left], 0)
    both = both.reshape(columns, CORES, half, rank)
    both = both.transpose(1, 2, 0, 3).reshape(CORES, half, columns * rank)
    both = (both.astype(jnp.float32) * DIAG_SCALE).astype(jnp.float16)

    def reduce(their_right, small):
        positions = jnp.arange(rank)
        kept = positions < diag_ranks[:, None, None]
        right = jnp.where(positions < tile_ranks[:, :, None, None], right_factors, 0)
        right = jnp.concatenate([right, their_right], 0)
        diag = jnp.concatenate([jnp.where(kept, diag_right, 0), small], 0)
        partial_product = jnp.einsum(
            "jmcr,jcs->mjsr", right, diag, preferred_element_type=jnp.float32
        )
        total = lax.psum((partial_product * CORE_SCALE).astype(jnp.float16), "tile")
        mine = lax.dynamic_index_in_dim(total, local_tile, 0, keepdims=False)
        core = (mine.astype(jnp.float32) * (1.0 / CORE_SCALE)).astype(jnp.bfloat16)
        return jnp.concatenate([core, left_factors.reshape(-1, rank, rank)], 0)

    def no_bundle(*_):
        blocks = columns + left_factors.size // (rank * rank)
        return jnp.zeros((blocks, rank, rank), jnp.bfloat16)

    def gather(both):
        rows = lax.all_gather(both, "tile", axis=1, tiled=True)
        return rows, jnp.full((1, 1), 1.0 / DIAG_SCALE, jnp.float32)

    def no_rows(_):
        shape = (CORES, half * tile_count, columns * rank)
        return jnp.zeros(shape, jnp.float16), jnp.zeros((1, 1), jnp.float32)

    bundle = lax.cond(gathers, no_bundle, reduce, their_right, small)
    bundle = lax.ppermute(bundle, "panel", to_first)
    rows, unit = lax.cond(gathers, gather, no_rows, both)

    smem = pl.BlockSpec(memory_space=pltpu.SMEM)
    vmem = pl.BlockSpec(memory_space=pltpu.VMEM)
    mixed = pl.pallas_call(
        mix_kernel,
        in_specs=[smem, smem, smem, vmem, vmem],
        out_specs=vmem,
        out_shape=jax.ShapeDtypeStruct((columns * rank, row_dev), jnp.bfloat16),
        cost_estimate=pl.CostEstimate(
            flops=2 * columns * rank * rank * row_dev, bytes_accessed=4 << 20, transcendentals=0
        ),
        compiler_params=pltpu.CompilerParams(vmem_limit_bytes=VMEM_BYTES),
        name="mix",
    )(local_tile.astype(jnp.int32)[None], tile_ranks, diag_ranks, bundle, left_factors)

    def expand(a):
        out = jnp.dot(rows[a].astype(jnp.bfloat16), mixed, preferred_element_type=jnp.float32)
        out = (out * unit).astype(jnp.bfloat16)
        return out.reshape(tile_count, half, row_dev)

    given = lax.ppermute(expand(1), "panel", to_second)
    terms = jnp.where(gathers, expand(0), given)
    parts = lax.all_to_all(
        terms, "panel", split_axis=0, concat_axis=0, tiled=True, axis_index_groups=across
    )
    delta = jnp.sum(parts.astype(jnp.float32), axis=0)
    return target - delta.T


def solution(mesh):
    placed = (
        P("tile", "panel"),
        P("panel", "tile", None),
        P("panel", None, "tile", None),
        P("panel", "tile", None),
        P("panel", "tile", None),
        P("panel", None),
        P("panel"),
    )
    return jax.shard_map(
        shards, mesh=mesh, in_specs=placed, out_specs=P("tile", "panel"), check_vma=False
    )
```

time: 136 us -> 130 us (0.956)
  starting transfers between devices: 21.9 us -> 12.8 us
  matrix products: 9.32 us -> 6.21 us
  other arithmetic: 3.71 us -> 6.35 us
  local copies, waits for them, and re-layouts: 0.86 us -> 2.64 us
    ppermute x4, starting transfers between devices: 21.9 us -> 12.8 us  [the longest x1 8.83 us: shards(): lax.ppermute(jnp.where(gathers, diag_right, diag_left), 'panel', swap)]
    dot_general x2 -> x1, matrix products: 5.76 us -> 2.64 us  [reduce(): jnp.einsum('jmcr,jcs->mjsr', right, diag, preferred_element_type=jnp.floa...]
where the time goes in v5:
time: 130 us
  blocking collectives  95.1 us (73%)
  starting transfers between devices  12.8 us (10%)
  other arithmetic  6.35 us (5%)
  matrix products  6.21 us (5%)
  waiting for transfers between devices  5.55 us (4%)
  local copies, waits for them, and re-layouts  2.64 us (2%)
    psum x1, blocking collectives, reduce(): total = lax.psum((partial_product * CORE_SCALE).astype(jnp.float16), 'tile')  72.6 us
    all_to_all x1, blocking collectives, shards(): lax.all_to_all(terms, 'panel', split_axis=0, concat_axis=0, tiled=True, a...  22.5 us
    ppermute x1, starting transfers between devices, shards(): lax.ppermute(jnp.where(gathers, diag_right, diag_left), 'panel', swap)  8.83 us
    dot_general x2, matrix products, expand(): jnp.dot(rows[a].astype(jnp.bfloat16), mixed, preferred_element_type=jnp.f...  3.56 us
    dot_general x1, matrix products, reduce(): jnp.einsum('jmcr,jcs->mjsr', right, diag, preferred_element_type=jnp.floa...  2.64 us
  transfers between devices with their start and end apart: 4, of which 3 were waited for; matrix products, arithmetic and copies ran while one was open for 2% of the time, Pallas kernels for 0%

profile of v5, /device:TPU:1, one launch (start us, length us, event | category | flops | bytes accessed | tf_op | source)
XLA Modules:
  0.0 130.0 jit_solution(17873176793267780793)
XLA Ops:
  0.0 1.3 collective-permute-start.1
  1.3 1.0 broadcast_select_fusion.3
  2.3 8.8 %collective-permute-start = (bf16[3,128,256]{2,1,0:T(8,128)(2,1)S(1)}, bf16[3,128,256]{2,1,0:T(8,128)(2,1)S(1)}, u32[]{:S(2)}, u32[]{:S(2)}) collective-permute-start(bf16[3,128,256]{2,1,0:T(8,128)(2,1)S(1)} %broadcast_select_fusion.3), channel_id=1, source_target_pairs={{0,16},{16,0},{32,48},{48,32},{64,80},{80,64},{96,112},{112,96},{1... | collective-permute-start | bytes 589832 | tf_op jit(solution)/shard_map/ppermute | solution.py:52
  11.1 1.0 collective-permute-done
  12.2 81.8 %conditional.3 = (bf16[12,256,256]{2,1,0:T(8,128)(2,1)}) conditional(s32[]{:T(128)} %convert_element_type.61, (s32[3]{0:T(128)}, bf16[3,128,256]{2,1,0:T(8,128)(2,1)}, bf16[3,128,256]{2,1,0:T(8,128)(2,1)S(1)}, s32[3,4]{1,0:T(4,128)}, bf16[3,4,128,256]{3,2,1,0:T(8,128)(2,1)}, /*index=5*/bf16[3,4,128,256]{3,2,1,0:T(8,128)(2,1)S(1)}, s32[]{:T(128)}, ...), branch_computations={%region_2.4_spmd, %region_4.5_spmd} | conditional | flops 412978944 | bytes 22027908 | solution.py:86
  12.2 0.8 iota_compare_fusion
  13.0 1.2 broadcast_select_fusion
  14.2 1.1 copy.14
  15.2 0.7 iota_compare_fusion.1
  16.3 2.6 %multiply_convert_fusion = f16[6,256,4,256]{3,1,2,0:T(8,128)(2,1)} fusion(bf16[3,4,128,256]{3,2,1,0:T(8,128)(2,1)S(1)} %get-tuple-element.30, bf16[3,4,128,256]{3,2,1,0:T(8,128)(2,1)S(1)} %broadcast_select_fusion, bf16[3,128,256]{1,2,0:T(8,128)(2,1)S(1)} %copy.15, bf16[3,128,256]{1,2,0:T(8,128)(2,1)S(1)} %broadcast_select_fusion.1), kind=kOutput, calls=%fused_computation | convolution fusion | flops 409731072 | bytes 5111808 | tf_op jit(solution)/shard_map/cond/branch_0_fun/jmcr,jcs->mjsr/dot_general | solution.py:66
  19.0 72.6 %all-reduce.1 = u32[4,6,4,8192]{3,2,0,1:T(4,128)S(1)} all-reduce(u32[4,6,4,8192]{3,2,0,1:T(4,128)} %bitcast.37), channel_id=1, replica_groups=mesh['panel'=32,'tile'=16] {'tile'}, use_global_device_ids=true, to_apply=%region_3.3.clone | all-reduce | flops 786432 | bytes 6291456 | tf_op jit(solution)/shard_map/cond/branch_0_fun/psum | solution.py:69
  91.8 0.9 copy-done.1
  92.7 1.3 pad_maximum_fusion
  94.0 1.4 %collective-permute-start.2 = (bf16[12,256,256]{2,1,0:T(8,128)(2,1)}, bf16[12,256,256]{2,1,0:T(8,128)(2,1)S(1)}, u32[]{:S(2)}, u32[]{:S(2)}) collective-permute-start(bf16[12,256,256]{2,1,0:T(8,128)(2,1)} %get-tuple-element.59), channel_id=1, source_target_pairs={{16,0},{48,32},{80,64},{112,96},{144,128},{176,160},{208,192},{240... | collective-permute-start | bytes 4718600 | tf_op jit(solution)/shard_map/ppermute | solution.py:87
  95.5 0.4 conditional.2
  95.5 0.4 broadcast.43
  96.0 2.5 %collective-permute-done.2.bundle = bf16[12,256,256]{2,1,0:T(8,128)(2,1)S(1)} collective-permute-done((bf16[12,256,256]{2,1,0:T(8,128)(2,1)}, bf16[12,256,256]{2,1,0:T(8,128)(2,1)S(1)}, u32[]{:S(2)}, u32[]{:S(2)}) %collective-permute-start.2) | collective-permute-done | bytes 1572896 | tf_op jit(solution)/shard_map/ppermute | solution.py:87
  98.5 1.2 mix.1
  99.7 1.8 %multiply_convert_fusion.2 = bf16[1024,512]{1,0:T(8,128)(2,1)S(1)} fusion(bf16[1536,512]{1,0:T(8,128)(2,1)S(1)} %mix.1, f16[2,1024,1536]{2,1,0:T(8,128)(2,1)S(1)} %get-tuple-element.35, f32[]{:T(128)} %bitcast.9), kind=kOutput, calls=%fused_computation.24 | convolution fusion | flops 1613234176 | bytes 5767172 | tf_op jit(solution)/shard_map/dot_general | solution.py:105
  101.5 1.3 collective-permute-start.3
  102.8 1.8 %multiply_convert_fusion.3 = bf16[1024,512]{1,0:T(8,128)(2,1)S(1)} fusion(bf16[1536,512]{1,0:T(8,128)(2,1)S(1)} %mix.1, f16[2,1024,1536]{2,1,0:T(8,128)(2,1)S(1)} %get-tuple-element.35, f32[]{:T(128)} %bitcast.9), kind=kOutput, calls=%fused_computation.25 | convolution fusion | flops 1613234176 | bytes 5767172 | tf_op jit(solution)/shard_map/dot_general | solution.py:105
  104.6 2.0 %collective-permute-done.3 = bf16[16,64,512]{2,1,0:T(8,128)(2,1)S(1)} collective-permute-done((bf16[16,64,512]{2,1,0:T(8,128)(2,1)S(1)}, bf16[16,64,512]{2,1,0:T(8,128)(2,1)S(1)}, u32[]{:S(2)}, u32[]{:S(2)}) %collective-permute-start.3) | collective-permute-done | bytes 1048608 | tf_op jit(solution)/shard_map/ppermute | solution.py:109
  106.7 22.5 %all_to_all.5 = bf16[16,64,512]{2,1,0:T(8,128)(2,1)S(1)} all-to-all(bf16[16,64,512]{2,1,0:T(8,128)(2,1)S(1)} %broadcast_select_fusion.2), channel_id=1, replica_groups={{0,32,64,96,128,160,192,224,256,288,320,352,384,416,448,480},{16,48,80,..., dimensions={0} | all-to-all | bytes 2097152 | tf_op jit(solution)/shard_map/all_to_all | solution.py:111
  129.3 0.7 bitcast_subtract_fusion
  (18 shorter events, 0.9 us)
Async XLA Ops:
  0.0 12.2 %collective-permute-start.1 = (bf16[3,4,128,256]{3,2,1,0:T(8,128)(2,1)}, bf16[3,4,128,256]{3,2,1,0:T(8,128)(2,1)S(1)}, u32[]{:S(2)}, u32[]{:S(2)}) collective-permute-start(bf16[3,4,128,256]{3,2,1,0:T(8,128)(2,1)} %param.13), channel_id=1, source_target_pairs={{0,16},{32,48},{64,80},{96,112},{128,144},{160,176},{192,208},{224... | collective-permute-start | bytes 2359304 | tf_op jit(solution)/shard_map/ppermute | solution.py:53
  2.3 9.9 %collective-permute-start = (bf16[3,128,256]{2,1,0:T(8,128)(2,1)S(1)}, bf16[3,128,256]{2,1,0:T(8,128)(2,1)S(1)}, u32[]{:S(2)}, u32[]{:S(2)}) collective-permute-start(bf16[3,128,256]{2,1,0:T(8,128)(2,1)S(1)} %broadcast_select_fusion.3), channel_id=1, source_target_pairs={{0,16},{16,0},{32,48},{48,32},{64,80},{80,64},{96,112},{112,96},{1... | collective-permute-start | bytes 589832 | tf_op jit(solution)/shard_map/ppermute | solution.py:52
  12.2 83.2 %copy-start.2 = (bf16[3,128,256]{2,1,0:T(8,128)(2,1)S(1)}, bf16[3,128,256]{2,1,0:T(8,128)(2,1)}, u32[]{:S(2)}) copy-start(bf16[3,128,256]{2,1,0:T(8,128)(2,1)} %param.14) | copy-start | bytes 589828
  91.6 1.1 copy-start.1
  94.0 4.5 %collective-permute-start.2 = (bf16[12,256,256]{2,1,0:T(8,128)(2,1)}, bf16[12,256,256]{2,1,0:T(8,128)(2,1)S(1)}, u32[]{:S(2)}, u32[]{:S(2)}) collective-permute-start(bf16[12,256,256]{2,1,0:T(8,128)(2,1)} %get-tuple-element.59), channel_id=1, source_target_pairs={{16,0},{48,32},{80,64},{112,96},{144,128},{176,160},{208,192},{240... | collective-permute-start | bytes 4718600 | tf_op jit(solution)/shard_map/ppermute | solution.py:87
  95.5 3.0 %copy-start = (bf16[3,512,256]{2,1,0:T(8,128)(2,1)S(1)}, bf16[3,512,256]{2,1,0:T(8,128)(2,1)}, u32[]{:S(2)}) copy-start(bf16[3,512,256]{2,1,0:T(8,128)(2,1)} %ours.1) | copy-start | bytes 2359300
  95.5 3.0 %copy-start.4 = (s32[3,4]{1,0:T(4,128)S(1)}, s32[3,4]{1,0:T(4,128)}, u32[]{:S(2)}) copy-start(s32[3,4]{1,0:T(4,128)} %tranks.1) | copy-start | bytes 148
  95.5 3.0 %copy-start.5 = (s32[3]{0:T(128)S(1)}, s32[3]{0:T(128)}, u32[]{:S(2)}) copy-start(s32[3]{0:T(128)} %dranks.1) | copy-start | bytes 40
  101.5 5.1 %collective-permute-start.3 = (bf16[16,64,512]{2,1,0:T(8,128)(2,1)S(1)}, bf16[16,64,512]{2,1,0:T(8,128)(2,1)S(1)}, u32[]{:S(2)}, u32[]{:S(2)}) collective-permute-start(bf16[16,64,512]{2,1,0:T(8,128)(2,1)S(1)} %bitcast.43), channel_id=1, source_target_pairs={{0,16},{32,48},{64,80},{96,112},{128,144},{160,176},{192,208},{224... | collective-permute-start | bytes 3145736 | tf_op jit(solution)/shard_map/ppermute | solution.py:109
  106.7 22.6 %copy-start.3 = (f32[512,64]{0,1:T(8,128)S(1)}, f32[512,64]{0,1:T(8,128)}, u32[]{:S(2)}) copy-start(f32[512,64]{0,1:T(8,128)} %param.11) | copy-start | bytes 393220

commit v6 on v5

--- a/solution.py
+++ b/solution.py
@@ -11,22 +11,34 @@
 VMEM_BYTES = 12 << 20
 
 
+def masked(core, j, place, tranks, dranks):
+    row = lax.broadcasted_iota(jnp.int32, core.shape, 0)
+    col = lax.broadcasted_iota(jnp.int32, core.shape, 1)
+    keep = (col < tranks[j, place[0]]) & (row < dranks[j])
+    return jnp.where(keep, core.astype(jnp.float32), 0.0).astype(core.dtype)
+
+
+def mask_kernel(place, tranks, dranks, cores, left, bundle):
+    columns, row_dev, rank = left.shape
+    blocks = row_dev // rank
+    for j in range(columns):
+        bundle[j] = masked(cores[j], j, place, tranks, dranks)
+    bundle[columns : CORES * columns] = cores[columns:]
+    for j in range(columns):
+        first = CORES * columns + j * blocks
+        bundle[first : first + blocks] = left[j].reshape(blocks, rank, rank)
+
+
 def mix_kernel(place, tranks, dranks, bundle, ours, mixed):
     columns, row_dev, rank = ours.shape
-    cores = CORES * columns
     blocks = row_dev // rank
-    row = lax.broadcasted_iota(jnp.int32, (rank, rank), 0)
-    col = lax.broadcasted_iota(jnp.int32, (rank, rank), 1)
-    for j in range(cores):
-        core = bundle[j]
-        if j < columns:
-            first = cores + blocks * j
-            left = bundle[first : first + blocks].reshape(row_dev, rank)
+    for j in range(CORES * columns):
+        mine = j - columns
+        if mine < 0:
+            first = CORES * columns + j * blocks
+            core, left = bundle[j], bundle[first : first + blocks].reshape(row_dev, rank)
         else:
-            mine = j - columns
-            keep = (col < tranks[mine, place[0]]) & (row < dranks[mine])
-            core = jnp.where(keep, core.astype(jnp.float32), 0.0).astype(core.dtype)
-            left = ours[mine]
+            core, left = masked(bundle[j], mine, place, tranks, dranks), ours[mine]
         part = lax.dot_general(
             core, left, (((1,), (1,)), ((), ())), preferred_element_type=jnp.float32
         )
@@ -57,23 +69,33 @@
     both = both.transpose(1, 2, 0, 3).reshape(CORES, half, columns * rank)
     both = (both.astype(jnp.float32) * DIAG_SCALE).astype(jnp.float16)
 
+    place = local_tile.astype(jnp.int32)[None]
+    smem = pl.BlockSpec(memory_space=pltpu.SMEM)
+    vmem = pl.BlockSpec(memory_space=pltpu.VMEM)
+    params = pltpu.CompilerParams(vmem_limit_bytes=VMEM_BYTES)
+
+    bundled = (columns + left_factors.size // (rank * rank), rank, rank)
+
     def reduce(their_right, small):
-        positions = jnp.arange(rank)
-        kept = positions < diag_ranks[:, None, None]
-        right = jnp.where(positions < tile_ranks[:, :, None, None], right_factors, 0)
-        right = jnp.concatenate([right, their_right], 0)
-        diag = jnp.concatenate([jnp.where(kept, diag_right, 0), small], 0)
+        right = jnp.concatenate([right_factors, their_right], 0)
+        diag = jnp.concatenate([diag_right, small], 0)
         partial_product = jnp.einsum(
             "jmcr,jcs->mjsr", right, diag, preferred_element_type=jnp.float32
         )
         total = lax.psum((partial_product * CORE_SCALE).astype(jnp.float16), "tile")
         mine = lax.dynamic_index_in_dim(total, local_tile, 0, keepdims=False)
-        core = (mine.astype(jnp.float32) * (1.0 / CORE_SCALE)).astype(jnp.bfloat16)
-        return jnp.concatenate([core, left_factors.reshape(-1, rank, rank)], 0)
+        mine = (mine.astype(jnp.float32) * (1.0 / CORE_SCALE)).astype(jnp.bfloat16)
+        return pl.pallas_call(
+            mask_kernel,
+            in_specs=[smem, smem, smem, vmem, vmem],
+            out_specs=vmem,
+            out_shape=jax.ShapeDtypeStruct(bundled, mine.dtype),
+            compiler_params=params,
+            name="mask",
+        )(place, tile_ranks, diag_ranks, mine, left_factors)
 
     def no_bundle(*_):
-        blocks = columns + left_factors.size // (rank * rank)
-        return jnp.zeros((blocks, rank, rank), jnp.bfloat16)
+        return jnp.zeros(bundled, jnp.bfloat16)
 
     def gather(both):
         rows = lax.all_gather(both, "tile", axis=1, tiled=True)
@@ -87,8 +109,6 @@
     bundle = lax.ppermute(bundle, "panel", to_first)
     rows, unit = lax.cond(gathers, gather, no_rows, both)
 
-    smem = pl.BlockSpec(memory_space=pltpu.SMEM)
-    vmem = pl.BlockSpec(memory_space=pltpu.VMEM)
     mixed = pl.pallas_call(
         mix_kernel,
         in_specs=[smem, smem, smem, vmem, vmem],
@@ -97,9 +117,9 @@
         cost_estimate=pl.CostEstimate(
             flops=2 * columns * rank * rank * row_dev, bytes_accessed=4 << 20, transcendentals=0
         ),
-        compiler_params=pltpu.CompilerParams(vmem_limit_bytes=VMEM_BYTES),
+        compiler_params=params,
         name="mix",
-    )(local_tile.astype(jnp.int32)[None], tile_ranks, diag_ranks, bundle, left_factors)
+    )(place, tile_ranks, diag_ranks, bundle, left_factors)
 
     def expand(a):
         out = jnp.dot(rows[a].astype(jnp.bfloat16), mixed, preferred_element_type=jnp.float32)

time: 130 us -> 130 us (level)
  other arithmetic: 6.35 us -> 2.16 us
  Pallas kernels: 1.17 us -> 3.03 us
    pallas_call x0 -> x1, Pallas kernels: none -> 1.86 us  [reduce(): pl.pallas_call(mask_kernel, in_specs=[smem, smem, smem, vmem, vmem], out_...]
    lt x2 -> x0, other arithmetic: 1.53 us -> none  [the longest x1 0.8 us: reduce(): positions < tile_ranks[:, :, None, None]]
    select_n x2 -> x0, other arithmetic: 1.37 us -> none  [the longest x1 1.2 us: reduce(): jnp.where(positions < tile_ranks[:, :, None, None], right_factors, 0)]
  transfers between devices with their start and end apart: 4 -> 4, of which waited for: 3 -> 3; matrix products, arithmetic and copies ran while one was open for 2% -> 3% of each run, Pallas kernels for 0% -> 0%
where the time goes in v6:
time: 130 us
  blocking collectives  95.7 us (74%)
  starting transfers between devices  12.8 us (10%)
  matrix products  7.35 us (6%)
  waiting for transfers between devices  5.66 us (4%)
  Pallas kernels  3.03 us (2%)
  local copies, waits for them, and re-layouts  2.67 us (2%)
  other arithmetic  2.16 us (2%)
    psum x1, blocking collectives, reduce(): total = lax.psum((partial_product * CORE_SCALE).astype(jnp.float16), 'tile')  73.2 us
    all_to_all x1, blocking collectives, shards(): lax.all_to_all(terms, 'panel', split_axis=0, concat_axis=0, tiled=True, a...  22.5 us
    ppermute x1, starting transfers between devices, shards(): lax.ppermute(jnp.where(gathers, diag_right, diag_left), 'panel', swap)  8.83 us
    dot_general x1, matrix products, reduce(): jnp.einsum('jmcr,jcs->mjsr', right, diag, preferred_element_type=jnp.floa...  3.78 us
    dot_general x2, matrix products, expand(): jnp.dot(rows[a].astype(jnp.bfloat16), mixed, preferred_element_type=jnp.f...  3.58 us
  transfers between devices with their start and end apart: 4, of which 3 were waited for; matrix products, arithmetic and copies ran while one was open for 3% of the time, Pallas kernels for 0%

profile of v6, /device:TPU:1, one launch (start us, length us, event | category | flops | bytes accessed | tf_op | source)
XLA Modules:
  0.0 129.5 jit_solution(9127446565163894073)
XLA Ops:
  0.0 1.3 collective-permute-start.1
  1.3 1.0 broadcast_select_fusion.1
  2.3 8.8 %collective-permute-start = (bf16[3,128,256]{2,1,0:T(8,128)(2,1)S(1)}, bf16[3,128,256]{2,1,0:T(8,128)(2,1)S(1)}, u32[]{:S(2)}, u32[]{:S(2)}) collective-permute-start(bf16[3,128,256]{2,1,0:T(8,128)(2,1)S(1)} %broadcast_select_fusion.1), channel_id=1, source_target_pairs={{0,16},{16,0},{32,48},{48,32},{64,80},{80,64},{96,112},{112,96},{1... | collective-permute-start | bytes 589832 | tf_op jit(solution)/shard_map/ppermute | solution.py:64
  11.1 1.0 collective-permute-done
  12.2 81.3 %conditional.3 = (bf16[12,256,256]{2,1,0:T(8,128)(2,1)}) conditional(s32[]{:T(128)} %convert_element_type.56, (bf16[3,128,256]{2,1,0:T(8,128)(2,1)}, bf16[3,128,256]{2,1,0:T(8,128)(2,1)S(1)}, bf16[3,4,128,256]{3,2,1,0:T(8,128)(2,1)}, bf16[3,4,128,256]{3,2,1,0:T(8,128)(2,1)S(1)}, s32[]{:T(128)}, /*index=5*/s32[1]{0:T(128)}, s32[3,4]{1,0:T(4,128)}, ...), branch_computations={%region_2.4_spmd, %region_4.5_spmd} | conditional | flops 409337856 | bytes 16908658 | solution.py:108
  12.2 1.1 copy.16
  13.3 0.2 copy.17
  13.5 3.8 %multiply_convert_fusion = f16[6,256,4,256]{3,1,0,2:T(8,128)(2,1)} fusion(bf16[3,128,256]{1,2,0:T(8,128)(2,1)S(1)} %copy.17, bf16[3,128,256]{1,2,0:T(8,128)(2,1)S(1)} %copy.16, bf16[3,4,128,256]{3,2,1,0:T(8,128)(2,1)S(1)} %get-tuple-element.33, bf16[3,4,128,256]{3,2,1,0:T(8,128)(2,1)} %get-tuple-element.32), kind=kOutput, calls=%fused_computation | convolution fusion | flops 407371776 | bytes 5111808 | tf_op jit(solution)/shard_map/cond/branch_0_fun/jmcr,jcs->mjsr/dot_general | solution.py:82
  17.2 73.2 %all-reduce.1 = u32[4,6,4,8192]{3,2,1,0:T(4,128)S(1)} all-reduce(u32[4,6,4,8192]{3,2,1,0:T(4,128)} %bitcast.34), channel_id=1, replica_groups=mesh['panel'=32,'tile'=16] {'tile'}, use_global_device_ids=true, to_apply=%region_3.3.clone | all-reduce | flops 786432 | bytes 6291456 | tf_op jit(solution)/shard_map/cond/branch_0_fun/psum | solution.py:85
  90.4 0.2 fusion.1.cores
  90.6 0.9 copy-done.1
  91.6 1.9 %mask.1 = bf16[12,256,256]{2,1,0:T(8,128)(2,1)} custom-call(s32[1]{0:T(128)} %get-tuple-element.27.place, s32[3,4]{1,0:T(4,128)S(1)} %copy-done.5, s32[3]{0:T(128)S(1)} %copy-done.7, bf16[6,256,256]{2,1,0:T(8,128)(2,1)S(1)} %fusion.1.cores, bf16[3,512,256]{2,1,0:T(8,128)(2,1)S(1)} %copy-done.1), custom_call_target="tpu_custom_call" | custom-call | tf_op jit(solution)/shard_map/cond/branch_0_fun/mask/pallas_call | solution.py:88
  93.4 1.4 %collective-permute-start.2 = (bf16[12,256,256]{2,1,0:T(8,128)(2,1)}, bf16[12,256,256]{2,1,0:T(8,128)(2,1)S(1)}, u32[]{:S(2)}, u32[]{:S(2)}) collective-permute-start(bf16[12,256,256]{2,1,0:T(8,128)(2,1)} %get-tuple-element.64), channel_id=1, source_target_pairs={{16,0},{48,32},{80,64},{112,96},{144,128},{176,160},{208,192},{240... | collective-permute-start | bytes 4718600 | tf_op jit(solution)/shard_map/ppermute | solution.py:109
  95.0 0.4 conditional.2
  95.0 0.4 broadcast.20
  95.4 2.5 %collective-permute-done.2.bundle = bf16[12,256,256]{2,1,0:T(8,128)(2,1)S(1)} collective-permute-done((bf16[12,256,256]{2,1,0:T(8,128)(2,1)}, bf16[12,256,256]{2,1,0:T(8,128)(2,1)S(1)}, u32[]{:S(2)}, u32[]{:S(2)}) %collective-permute-start.2) | collective-permute-done | bytes 1572896 | tf_op jit(solution)/shard_map/ppermute | solution.py:109
  97.9 1.2 mix.1
  99.1 1.8 %multiply_convert_fusion.2 = bf16[1024,512]{1,0:T(8,128)(2,1)S(1)} fusion(bf16[1536,512]{1,0:T(8,128)(2,1)S(1)} %mix.1, f16[2,1024,1536]{2,1,0:T(8,128)(2,1)S(1)} %get-tuple-element.38, f32[]{:T(128)} %bitcast.7), kind=kOutput, calls=%fused_computation.18 | convolution fusion | flops 1613234176 | bytes 5767172 | tf_op jit(solution)/shard_map/dot_general | solution.py:125
  100.9 1.3 collective-permute-start.3
  102.2 1.8 %multiply_convert_fusion.3 = bf16[1024,512]{1,0:T(8,128)(2,1)S(1)} fusion(bf16[1536,512]{1,0:T(8,128)(2,1)S(1)} %mix.1, f16[2,1024,1536]{2,1,0:T(8,128)(2,1)S(1)} %get-tuple-element.38, f32[]{:T(128)} %bitcast.7), kind=kOutput, calls=%fused_computation.19 | convolution fusion | flops 1613234176 | bytes 5767172 | tf_op jit(solution)/shard_map/dot_general | solution.py:125
  104.0 2.1 %collective-permute-done.3 = bf16[16,64,512]{2,1,0:T(8,128)(2,1)S(1)} collective-permute-done((bf16[16,64,512]{2,1,0:T(8,128)(2,1)S(1)}, bf16[16,64,512]{2,1,0:T(8,128)(2,1)S(1)}, u32[]{:S(2)}, u32[]{:S(2)}) %collective-permute-start.3) | collective-permute-done | bytes 1048608 | tf_op jit(solution)/shard_map/ppermute | solution.py:129
  106.2 22.5 %all_to_all.5 = bf16[16,64,512]{2,1,0:T(8,128)(2,1)S(1)} all-to-all(bf16[16,64,512]{2,1,0:T(8,128)(2,1)S(1)} %broadcast_select_fusion), channel_id=1, replica_groups={{0,32,64,96,128,160,192,224,256,288,320,352,384,416,448,480},{16,48,80,..., dimensions={0} | all-to-all | bytes 2097152 | tf_op jit(solution)/shard_map/all_to_all | solution.py:131
  128.7 0.1 convert_reduce_fusion
  128.9 0.7 bitcast_subtract_fusion
  (18 shorter events, 0.2 us)
Async XLA Ops:
  0.0 12.2 %collective-permute-start.1 = (bf16[3,4,128,256]{3,2,1,0:T(8,128)(2,1)}, bf16[3,4,128,256]{3,2,1,0:T(8,128)(2,1)S(1)}, u32[]{:S(2)}, u32[]{:S(2)}) collective-permute-start(bf16[3,4,128,256]{3,2,1,0:T(8,128)(2,1)} %param.13), channel_id=1, source_target_pairs={{0,16},{32,48},{64,80},{96,112},{128,144},{160,176},{192,208},{224... | collective-permute-start | bytes 2359304 | tf_op jit(solution)/shard_map/ppermute | solution.py:65
  2.3 9.9 %collective-permute-start = (bf16[3,128,256]{2,1,0:T(8,128)(2,1)S(1)}, bf16[3,128,256]{2,1,0:T(8,128)(2,1)S(1)}, u32[]{:S(2)}, u32[]{:S(2)}) collective-permute-start(bf16[3,128,256]{2,1,0:T(8,128)(2,1)S(1)} %broadcast_select_fusion.1), channel_id=1, source_target_pairs={{0,16},{16,0},{32,48},{48,32},{64,80},{80,64},{96,112},{112,96},{1... | collective-permute-start | bytes 589832 | tf_op jit(solution)/shard_map/ppermute | solution.py:64
  12.2 82.7 %copy-start.2 = (bf16[3,128,256]{2,1,0:T(8,128)(2,1)S(1)}, bf16[3,128,256]{2,1,0:T(8,128)(2,1)}, u32[]{:S(2)}) copy-start(bf16[3,128,256]{2,1,0:T(8,128)(2,1)} %param.14) | copy-start | bytes 589828
  17.2 73.4 %copy-start.5 = (s32[3,4]{1,0:T(4,128)S(1)}, s32[3,4]{1,0:T(4,128)}, u32[]{:S(2)}) copy-start(s32[3,4]{1,0:T(4,128)} %get-tuple-element.28.tranks) | copy-start | bytes 148 | tf_op jit(solution)/shard_map/cond
  17.2 73.4 %copy-start.7 = (s32[3]{0:T(128)S(1)}, s32[3]{0:T(128)}, u32[]{:S(2)}) copy-start(s32[3]{0:T(128)} %get-tuple-element.29.dranks) | copy-start | bytes 40 | tf_op jit(solution)/shard_map/cond
  90.4 1.1 copy-start.1
  93.4 4.5 %collective-permute-start.2 = (bf16[12,256,256]{2,1,0:T(8,128)(2,1)}, bf16[12,256,256]{2,1,0:T(8,128)(2,1)S(1)}, u32[]{:S(2)}, u32[]{:S(2)}) collective-permute-start(bf16[12,256,256]{2,1,0:T(8,128)(2,1)} %get-tuple-element.64), channel_id=1, source_target_pairs={{16,0},{48,32},{80,64},{112,96},{144,128},{176,160},{208,192},{240... | collective-permute-start | bytes 4718600 | tf_op jit(solution)/shard_map/ppermute | solution.py:109
  94.9 3.0 %copy-start = (bf16[3,512,256]{2,1,0:T(8,128)(2,1)S(1)}, bf16[3,512,256]{2,1,0:T(8,128)(2,1)}, u32[]{:S(2)}) copy-start(bf16[3,512,256]{2,1,0:T(8,128)(2,1)} %ours.1) | copy-start | bytes 2359300
  94.9 3.0 %copy-start.4 = (s32[3,4]{1,0:T(4,128)S(1)}, s32[3,4]{1,0:T(4,128)}, u32[]{:S(2)}) copy-start(s32[3,4]{1,0:T(4,128)} %tranks.1) | copy-start | bytes 148
  94.9 3.0 %copy-start.6 = (s32[3]{0:T(128)S(1)}, s32[3]{0:T(128)}, u32[]{:S(2)}) copy-start(s32[3]{0:T(128)} %dranks.1) | copy-start | bytes 40
  100.9 5.2 %collective-permute-start.3 = (bf16[16,64,512]{2,1,0:T(8,128)(2,1)S(1)}, bf16[16,64,512]{2,1,0:T(8,128)(2,1)S(1)}, u32[]{:S(2)}, u32[]{:S(2)}) collective-permute-start(bf16[16,64,512]{2,1,0:T(8,128)(2,1)S(1)} %bitcast.39), channel_id=1, source_target_pairs={{0,16},{32,48},{64,80},{96,112},{128,144},{160,176},{192,208},{224... | collective-permute-start | bytes 3145736 | tf_op jit(solution)/shard_map/ppermute | solution.py:129
  106.2 22.6 %copy-start.3 = (f32[512,64]{0,1:T(8,128)S(1)}, f32[512,64]{0,1:T(8,128)}, u32[]{:S(2)}) copy-start(f32[512,64]{0,1:T(8,128)} %param.11) | copy-start | bytes 393220

commit v7 on v6

--- a/solution.py
+++ b/solution.py
@@ -131,8 +131,10 @@
     parts = lax.all_to_all(
         terms, "panel", split_axis=0, concat_axis=0, tiled=True, axis_index_groups=across
     )
-    delta = jnp.sum(parts.astype(jnp.float32), axis=0)
-    return target - delta.T
+    rest = target.T
+    for part in range(chip_count):
+        rest = rest - parts[part].astype(jnp.float32)
+    return rest.T
 
 
 def solution(mesh):

time: 130 us -> 130 us (level)
  no operation moved by 1% of the time
where the time goes in v7:
time: 130 us; the launch traced here: 129 us
  blocking collectives  95.5 us (73%)
  starting transfers between devices  12.8 us (10%)
  matrix products  7.35 us (6%)
  waiting for transfers between devices  5.66 us (4%)
  Pallas kernels  3.03 us (2%)
  local copies, waits for them, and re-layouts  2.66 us (2%)
  other arithmetic  2.15 us (2%)
    psum x1, blocking collectives, reduce(): total = lax.psum((partial_product * CORE_SCALE).astype(jnp.float16), 'tile')  73.2 us
    all_to_all x1, blocking collectives, shards(): lax.all_to_all(terms, 'panel', split_axis=0, concat_axis=0, tiled=True, a...  22.4 us
    ppermute x1, starting transfers between devices, shards(): lax.ppermute(jnp.where(gathers, diag_right, diag_left), 'panel', swap)  8.83 us
    dot_general x1, matrix products, reduce(): jnp.einsum('jmcr,jcs->mjsr', right, diag, preferred_element_type=jnp.floa...  3.78 us
    dot_general x2, matrix products, expand(): jnp.dot(rows[a].astype(jnp.bfloat16), mixed, preferred_element_type=jnp.f...  3.58 us
  transfers between devices with their start and end apart: 4, of which 3 were waited for; matrix products, arithmetic and copies ran while one was open for 3% of the time, Pallas kernels for 0%

profile of v7, /device:TPU:1, one launch (start us, length us, event | category | flops | bytes accessed | tf_op | source)
XLA Modules:
  0.0 129.4 jit_solution(10420012197970698169)
XLA Ops:
  0.0 1.3 collective-permute-start.1
  1.3 1.0 broadcast_select_fusion.1
  2.3 8.8 %collective-permute-start = (bf16[3,128,256]{2,1,0:T(8,128)(2,1)S(1)}, bf16[3,128,256]{2,1,0:T(8,128)(2,1)S(1)}, u32[]{:S(2)}, u32[]{:S(2)}) collective-permute-start(bf16[3,128,256]{2,1,0:T(8,128)(2,1)S(1)} %broadcast_select_fusion.1), channel_id=1, source_target_pairs={{0,16},{16,0},{32,48},{48,32},{64,80},{80,64},{96,112},{112,96},{1... | collective-permute-start | bytes 589832 | tf_op jit(solution)/shard_map/ppermute | solution.py:64
  11.1 1.0 collective-permute-done
  12.2 81.3 %conditional.3 = (bf16[12,256,256]{2,1,0:T(8,128)(2,1)}) conditional(s32[]{:T(128)} %convert_element_type.149, (bf16[3,128,256]{2,1,0:T(8,128)(2,1)}, bf16[3,128,256]{2,1,0:T(8,128)(2,1)S(1)}, bf16[3,4,128,256]{3,2,1,0:T(8,128)(2,1)}, bf16[3,4,128,256]{3,2,1,0:T(8,128)(2,1)S(1)}, s32[]{:T(128)}, /*index=5*/s32[1]{0:T(128)}, s32[3,4]{1,0:T(4,128)}, ...), branch_computations={%region_2.4_spmd, %region_4.5_spmd} | conditional | flops 409337856 | bytes 16908658 | solution.py:108
  12.2 1.1 copy.16
  13.3 0.2 copy.17
  13.5 3.8 %multiply_convert_fusion = f16[6,256,4,256]{3,1,0,2:T(8,128)(2,1)} fusion(bf16[3,128,256]{1,2,0:T(8,128)(2,1)S(1)} %copy.17, bf16[3,128,256]{1,2,0:T(8,128)(2,1)S(1)} %copy.16, bf16[3,4,128,256]{3,2,1,0:T(8,128)(2,1)S(1)} %get-tuple-element.33, bf16[3,4,128,256]{3,2,1,0:T(8,128)(2,1)} %get-tuple-element.32), kind=kOutput, calls=%fused_computation | convolution fusion | flops 407371776 | bytes 5111808 | tf_op jit(solution)/shard_map/cond/branch_0_fun/jmcr,jcs->mjsr/dot_general | solution.py:82
  17.2 73.2 %all-reduce.1 = u32[4,6,4,8192]{3,2,1,0:T(4,128)S(1)} all-reduce(u32[4,6,4,8192]{3,2,1,0:T(4,128)} %bitcast.116), channel_id=1, replica_groups=mesh['panel'=32,'tile'=16] {'tile'}, use_global_device_ids=true, to_apply=%region_3.3.clone | all-reduce | flops 786432 | bytes 6291456 | tf_op jit(solution)/shard_map/cond/branch_0_fun/psum | solution.py:85
  90.4 0.2 fusion.1.cores
  90.6 0.9 copy-done.1
  91.6 1.9 %mask.1 = bf16[12,256,256]{2,1,0:T(8,128)(2,1)} custom-call(s32[1]{0:T(128)} %get-tuple-element.27.place, s32[3,4]{1,0:T(4,128)S(1)} %copy-done.5, s32[3]{0:T(128)S(1)} %copy-done.7, bf16[6,256,256]{2,1,0:T(8,128)(2,1)S(1)} %fusion.1.cores, bf16[3,512,256]{2,1,0:T(8,128)(2,1)S(1)} %copy-done.1), custom_call_target="tpu_custom_call" | custom-call | tf_op jit(solution)/shard_map/cond/branch_0_fun/mask/pallas_call | solution.py:88
  93.4 1.4 %collective-permute-start.2 = (bf16[12,256,256]{2,1,0:T(8,128)(2,1)}, bf16[12,256,256]{2,1,0:T(8,128)(2,1)S(1)}, u32[]{:S(2)}, u32[]{:S(2)}) collective-permute-start(bf16[12,256,256]{2,1,0:T(8,128)(2,1)} %get-tuple-element.64), channel_id=1, source_target_pairs={{16,0},{48,32},{80,64},{112,96},{144,128},{176,160},{208,192},{240... | collective-permute-start | bytes 4718600 | tf_op jit(solution)/shard_map/ppermute | solution.py:109
  95.0 0.4 conditional.2
  95.0 0.4 broadcast.20
  95.4 2.5 %collective-permute-done.2.bundle = bf16[12,256,256]{2,1,0:T(8,128)(2,1)S(1)} collective-permute-done((bf16[12,256,256]{2,1,0:T(8,128)(2,1)}, bf16[12,256,256]{2,1,0:T(8,128)(2,1)S(1)}, u32[]{:S(2)}, u32[]{:S(2)}) %collective-permute-start.2) | collective-permute-done | bytes 1572896 | tf_op jit(solution)/shard_map/ppermute | solution.py:109
  97.9 1.2 mix.1
  99.1 1.8 %multiply_convert_fusion.2 = bf16[1024,512]{1,0:T(8,128)(2,1)S(1)} fusion(bf16[1536,512]{1,0:T(8,128)(2,1)S(1)} %mix.1, f16[2,1024,1536]{2,1,0:T(8,128)(2,1)S(1)} %get-tuple-element.38, f32[]{:T(128)} %bitcast.8), kind=kOutput, calls=%fused_computation.17 | convolution fusion | flops 1613234176 | bytes 5767172 | tf_op jit(solution)/shard_map/dot_general | solution.py:125
  100.9 1.3 collective-permute-start.3
  102.2 1.8 %multiply_convert_fusion.3 = bf16[1024,512]{1,0:T(8,128)(2,1)S(1)} fusion(bf16[1536,512]{1,0:T(8,128)(2,1)S(1)} %mix.1, f16[2,1024,1536]{2,1,0:T(8,128)(2,1)S(1)} %get-tuple-element.38, f32[]{:T(128)} %bitcast.8), kind=kOutput, calls=%fused_computation.18 | convolution fusion | flops 1613234176 | bytes 5767172 | tf_op jit(solution)/shard_map/dot_general | solution.py:125
  104.0 2.1 %collective-permute-done.3 = bf16[16,64,512]{2,1,0:T(8,128)(2,1)S(1)} collective-permute-done((bf16[16,64,512]{2,1,0:T(8,128)(2,1)S(1)}, bf16[16,64,512]{2,1,0:T(8,128)(2,1)S(1)}, u32[]{:S(2)}, u32[]{:S(2)}) %collective-permute-start.3) | collective-permute-done | bytes 1048608 | tf_op jit(solution)/shard_map/ppermute | solution.py:129
  106.1 0.1 broadcast_select_fusion
  106.2 22.4 %all_to_all.5 = bf16[16,64,512]{2,1,0:T(8,128)(2,1)S(1)} all-to-all(bf16[16,64,512]{2,1,0:T(8,128)(2,1)S(1)} %broadcast_select_fusion), channel_id=1, replica_groups={{0,32,64,96,128,160,192,224,256,288,320,352,384,416,448,480},{16,48,80,..., dimensions={0} | all-to-all | bytes 2097152 | tf_op jit(solution)/shard_map/all_to_all | solution.py:131
  128.6 0.8 fusion.17
  (17 shorter events, 0.1 us)
Async XLA Ops:
  0.0 12.2 %collective-permute-start.1 = (bf16[3,4,128,256]{3,2,1,0:T(8,128)(2,1)}, bf16[3,4,128,256]{3,2,1,0:T(8,128)(2,1)S(1)}, u32[]{:S(2)}, u32[]{:S(2)}) collective-permute-start(bf16[3,4,128,256]{3,2,1,0:T(8,128)(2,1)} %param.13), channel_id=1, source_target_pairs={{0,16},{32,48},{64,80},{96,112},{128,144},{160,176},{192,208},{224... | collective-permute-start | bytes 2359304 | tf_op jit(solution)/shard_map/ppermute | solution.py:65
  2.3 9.9 %collective-permute-start = (bf16[3,128,256]{2,1,0:T(8,128)(2,1)S(1)}, bf16[3,128,256]{2,1,0:T(8,128)(2,1)S(1)}, u32[]{:S(2)}, u32[]{:S(2)}) collective-permute-start(bf16[3,128,256]{2,1,0:T(8,128)(2,1)S(1)} %broadcast_select_fusion.1), channel_id=1, source_target_pairs={{0,16},{16,0},{32,48},{48,32},{64,80},{80,64},{96,112},{112,96},{1... | collective-permute-start | bytes 589832 | tf_op jit(solution)/shard_map/ppermute | solution.py:64
  12.2 82.7 %copy-start.2 = (bf16[3,128,256]{2,1,0:T(8,128)(2,1)S(1)}, bf16[3,128,256]{2,1,0:T(8,128)(2,1)}, u32[]{:S(2)}) copy-start(bf16[3,128,256]{2,1,0:T(8,128)(2,1)} %param.14) | copy-start | bytes 589828
  17.2 73.4 %copy-start.5 = (s32[3,4]{1,0:T(4,128)S(1)}, s32[3,4]{1,0:T(4,128)}, u32[]{:S(2)}) copy-start(s32[3,4]{1,0:T(4,128)} %get-tuple-element.28.tranks) | copy-start | bytes 148 | tf_op jit(solution)/shard_map/cond
  17.2 73.4 %copy-start.7 = (s32[3]{0:T(128)S(1)}, s32[3]{0:T(128)}, u32[]{:S(2)}) copy-start(s32[3]{0:T(128)} %get-tuple-element.29.dranks) | copy-start | bytes 40 | tf_op jit(solution)/shard_map/cond
  90.4 1.1 copy-start.1
  93.4 4.5 %collective-permute-start.2 = (bf16[12,256,256]{2,1,0:T(8,128)(2,1)}, bf16[12,256,256]{2,1,0:T(8,128)(2,1)S(1)}, u32[]{:S(2)}, u32[]{:S(2)}) collective-permute-start(bf16[12,256,256]{2,1,0:T(8,128)(2,1)} %get-tuple-element.64), channel_id=1, source_target_pairs={{16,0},{48,32},{80,64},{112,96},{144,128},{176,160},{208,192},{240... | collective-permute-start | bytes 4718600 | tf_op jit(solution)/shard_map/ppermute | solution.py:109
  94.9 3.0 %copy-start = (bf16[3,512,256]{2,1,0:T(8,128)(2,1)S(1)}, bf16[3,512,256]{2,1,0:T(8,128)(2,1)}, u32[]{:S(2)}) copy-start(bf16[3,512,256]{2,1,0:T(8,128)(2,1)} %ours.1) | copy-start | bytes 2359300
  94.9 3.0 %copy-start.4 = (s32[3,4]{1,0:T(4,128)S(1)}, s32[3,4]{1,0:T(4,128)}, u32[]{:S(2)}) copy-start(s32[3,4]{1,0:T(4,128)} %tranks.1) | copy-start | bytes 148
  94.9 3.0 %copy-start.6 = (s32[3]{0:T(128)S(1)}, s32[3]{0:T(128)}, u32[]{:S(2)}) copy-start(s32[3]{0:T(128)} %dranks.1) | copy-start | bytes 40
  100.9 5.2 %collective-permute-start.3 = (bf16[16,64,512]{2,1,0:T(8,128)(2,1)S(1)}, bf16[16,64,512]{2,1,0:T(8,128)(2,1)S(1)}, u32[]{:S(2)}, u32[]{:S(2)}) collective-permute-start(bf16[16,64,512]{2,1,0:T(8,128)(2,1)S(1)} %bitcast.121), channel_id=1, source_target_pairs={{0,16},{32,48},{64,80},{96,112},{128,144},{160,176},{192,208},{224... | collective-permute-start | bytes 3145736 | tf_op jit(solution)/shard_map/ppermute | solution.py:129
  106.1 22.5 %copy-start.3 = (f32[512,64]{0,1:T(8,128)S(1)}, f32[512,64]{0,1:T(8,128)}, u32[]{:S(2)}) copy-start(f32[512,64]{0,1:T(8,128)} %param.11) | copy-start | bytes 393220

commit v8 on v7

--- a/solution.py
+++ b/solution.py
@@ -8,7 +8,7 @@
 CORES = 2
 CORE_SCALE = 2.0**10
 DIAG_SCALE = 2.0**15
-VMEM_BYTES = 12 << 20
+VMEM_BYTES = 7 << 20
 
 
 def masked(core, j, place, tranks, dranks):

time: 130 us -> 130 us (level)
  no operation moved by 1% of the time
where the time goes in v8:
time: 130 us; the launch traced here: 129 us
  blocking collectives  95.5 us (73%)
  starting transfers between devices  12.8 us (10%)
  matrix products  7.35 us (6%)
  waiting for transfers between devices  5.66 us (4%)
  Pallas kernels  3.03 us (2%)
  local copies, waits for them, and re-layouts  2.66 us (2%)
  other arithmetic  2.15 us (2%)
    psum x1, blocking collectives, reduce(): total = lax.psum((partial_product * CORE_SCALE).astype(jnp.float16), 'tile')  73.2 us
    all_to_all x1, blocking collectives, shards(): lax.all_to_all(terms, 'panel', split_axis=0, concat_axis=0, tiled=True, a...  22.4 us
    ppermute x1, starting transfers between devices, shards(): lax.ppermute(jnp.where(gathers, diag_right, diag_left), 'panel', swap)  8.83 us
    dot_general x1, matrix products, reduce(): jnp.einsum('jmcr,jcs->mjsr', right, diag, preferred_element_type=jnp.floa...  3.78 us
    dot_general x2, matrix products, expand(): jnp.dot(rows[a].astype(jnp.bfloat16), mixed, preferred_element_type=jnp.f...  3.58 us
  transfers between devices with their start and end apart: 4, of which 3 were waited for; matrix products, arithmetic and copies ran while one was open for 3% of the time, Pallas kernels for 0%

profile of v8, /device:TPU:1, one launch (start us, length us, event | category | flops | bytes accessed | tf_op | source)
XLA Modules:
  0.0 129.4 jit_solution(10420012197970698169)
XLA Ops:
  0.0 1.3 collective-permute-start.1
  1.3 1.0 broadcast_select_fusion.1
  2.3 8.8 %collective-permute-start = (bf16[3,128,256]{2,1,0:T(8,128)(2,1)S(1)}, bf16[3,128,256]{2,1,0:T(8,128)(2,1)S(1)}, u32[]{:S(2)}, u32[]{:S(2)}) collective-permute-start(bf16[3,128,256]{2,1,0:T(8,128)(2,1)S(1)} %broadcast_select_fusion.1), channel_id=1, source_target_pairs={{0,16},{16,0},{32,48},{48,32},{64,80},{80,64},{96,112},{112,96},{1... | collective-permute-start | bytes 589832 | tf_op jit(solution)/shard_map/ppermute | solution.py:64
  11.1 1.0 collective-permute-done
  12.2 81.3 %conditional.3 = (bf16[12,256,256]{2,1,0:T(8,128)(2,1)}) conditional(s32[]{:T(128)} %convert_element_type.149, (bf16[3,128,256]{2,1,0:T(8,128)(2,1)}, bf16[3,128,256]{2,1,0:T(8,128)(2,1)S(1)}, bf16[3,4,128,256]{3,2,1,0:T(8,128)(2,1)}, bf16[3,4,128,256]{3,2,1,0:T(8,128)(2,1)S(1)}, s32[]{:T(128)}, /*index=5*/s32[1]{0:T(128)}, s32[3,4]{1,0:T(4,128)}, ...), branch_computations={%region_2.4_spmd, %region_4.5_spmd} | conditional | flops 409337856 | bytes 16908658 | solution.py:108
  12.2 1.1 copy.16
  13.3 0.2 copy.17
  13.5 3.8 %multiply_convert_fusion = f16[6,256,4,256]{3,1,0,2:T(8,128)(2,1)} fusion(bf16[3,128,256]{1,2,0:T(8,128)(2,1)S(1)} %copy.17, bf16[3,128,256]{1,2,0:T(8,128)(2,1)S(1)} %copy.16, bf16[3,4,128,256]{3,2,1,0:T(8,128)(2,1)S(1)} %get-tuple-element.33, bf16[3,4,128,256]{3,2,1,0:T(8,128)(2,1)} %get-tuple-element.32), kind=kOutput, calls=%fused_computation | convolution fusion | flops 407371776 | bytes 5111808 | tf_op jit(solution)/shard_map/cond/branch_0_fun/jmcr,jcs->mjsr/dot_general | solution.py:82
  17.2 73.2 %all-reduce.1 = u32[4,6,4,8192]{3,2,1,0:T(4,128)S(1)} all-reduce(u32[4,6,4,8192]{3,2,1,0:T(4,128)} %bitcast.116), channel_id=1, replica_groups=mesh['panel'=32,'tile'=16] {'tile'}, use_global_device_ids=true, to_apply=%region_3.3.clone | all-reduce | flops 786432 | bytes 6291456 | tf_op jit(solution)/shard_map/cond/branch_0_fun/psum | solution.py:85
  90.4 0.2 fusion.1.cores
  90.6 0.9 copy-done.1
  91.6 1.9 %mask.1 = bf16[12,256,256]{2,1,0:T(8,128)(2,1)} custom-call(s32[1]{0:T(128)} %get-tuple-element.27.place, s32[3,4]{1,0:T(4,128)S(1)} %copy-done.5, s32[3]{0:T(128)S(1)} %copy-done.7, bf16[6,256,256]{2,1,0:T(8,128)(2,1)S(1)} %fusion.1.cores, bf16[3,512,256]{2,1,0:T(8,128)(2,1)S(1)} %copy-done.1), custom_call_target="tpu_custom_call" | custom-call | tf_op jit(solution)/shard_map/cond/branch_0_fun/mask/pallas_call | solution.py:88
  93.4 1.4 %collective-permute-start.2 = (bf16[12,256,256]{2,1,0:T(8,128)(2,1)}, bf16[12,256,256]{2,1,0:T(8,128)(2,1)S(1)}, u32[]{:S(2)}, u32[]{:S(2)}) collective-permute-start(bf16[12,256,256]{2,1,0:T(8,128)(2,1)} %get-tuple-element.64), channel_id=1, source_target_pairs={{16,0},{48,32},{80,64},{112,96},{144,128},{176,160},{208,192},{240... | collective-permute-start | bytes 4718600 | tf_op jit(solution)/shard_map/ppermute | solution.py:109
  95.0 0.4 conditional.2
  95.0 0.4 broadcast.20
  95.4 2.5 %collective-permute-done.2.bundle = bf16[12,256,256]{2,1,0:T(8,128)(2,1)S(1)} collective-permute-done((bf16[12,256,256]{2,1,0:T(8,128)(2,1)}, bf16[12,256,256]{2,1,0:T(8,128)(2,1)S(1)}, u32[]{:S(2)}, u32[]{:S(2)}) %collective-permute-start.2) | collective-permute-done | bytes 1572896 | tf_op jit(solution)/shard_map/ppermute | solution.py:109
  97.9 1.2 mix.1
  99.1 1.8 %multiply_convert_fusion.2 = bf16[1024,512]{1,0:T(8,128)(2,1)S(1)} fusion(bf16[1536,512]{1,0:T(8,128)(2,1)S(1)} %mix.1, f16[2,1024,1536]{2,1,0:T(8,128)(2,1)S(1)} %get-tuple-element.38, f32[]{:T(128)} %bitcast.8), kind=kOutput, calls=%fused_computation.17 | convolution fusion | flops 1613234176 | bytes 5767172 | tf_op jit(solution)/shard_map/dot_general | solution.py:125
  100.9 1.3 collective-permute-start.3
  102.2 1.8 %multiply_convert_fusion.3 = bf16[1024,512]{1,0:T(8,128)(2,1)S(1)} fusion(bf16[1536,512]{1,0:T(8,128)(2,1)S(1)} %mix.1, f16[2,1024,1536]{2,1,0:T(8,128)(2,1)S(1)} %get-tuple-element.38, f32[]{:T(128)} %bitcast.8), kind=kOutput, calls=%fused_computation.18 | convolution fusion | flops 1613234176 | bytes 5767172 | tf_op jit(solution)/shard_map/dot_general | solution.py:125
  104.0 2.1 %collective-permute-done.3 = bf16[16,64,512]{2,1,0:T(8,128)(2,1)S(1)} collective-permute-done((bf16[16,64,512]{2,1,0:T(8,128)(2,1)S(1)}, bf16[16,64,512]{2,1,0:T(8,128)(2,1)S(1)}, u32[]{:S(2)}, u32[]{:S(2)}) %collective-permute-start.3) | collective-permute-done | bytes 1048608 | tf_op jit(solution)/shard_map/ppermute | solution.py:129
  106.1 0.1 broadcast_select_fusion
  106.2 22.4 %all_to_all.5 = bf16[16,64,512]{2,1,0:T(8,128)(2,1)S(1)} all-to-all(bf16[16,64,512]{2,1,0:T(8,128)(2,1)S(1)} %broadcast_select_fusion), channel_id=1, replica_groups={{0,32,64,96,128,160,192,224,256,288,320,352,384,416,448,480},{16,48,80,..., dimensions={0} | all-to-all | bytes 2097152 | tf_op jit(solution)/shard_map/all_to_all | solution.py:131
  128.6 0.8 fusion.17
  (17 shorter events, 0.1 us)
Async XLA Ops:
  0.0 12.2 %collective-permute-start.1 = (bf16[3,4,128,256]{3,2,1,0:T(8,128)(2,1)}, bf16[3,4,128,256]{3,2,1,0:T(8,128)(2,1)S(1)}, u32[]{:S(2)}, u32[]{:S(2)}) collective-permute-start(bf16[3,4,128,256]{3,2,1,0:T(8,128)(2,1)} %param.13), channel_id=1, source_target_pairs={{0,16},{32,48},{64,80},{96,112},{128,144},{160,176},{192,208},{224... | collective-permute-start | bytes 2359304 | tf_op jit(solution)/shard_map/ppermute | solution.py:65
  2.3 9.9 %collective-permute-start = (bf16[3,128,256]{2,1,0:T(8,128)(2,1)S(1)}, bf16[3,128,256]{2,1,0:T(8,128)(2,1)S(1)}, u32[]{:S(2)}, u32[]{:S(2)}) collective-permute-start(bf16[3,128,256]{2,1,0:T(8,128)(2,1)S(1)} %broadcast_select_fusion.1), channel_id=1, source_target_pairs={{0,16},{16,0},{32,48},{48,32},{64,80},{80,64},{96,112},{112,96},{1... | collective-permute-start | bytes 589832 | tf_op jit(solution)/shard_map/ppermute | solution.py:64
  12.2 82.7 %copy-start.2 = (bf16[3,128,256]{2,1,0:T(8,128)(2,1)S(1)}, bf16[3,128,256]{2,1,0:T(8,128)(2,1)}, u32[]{:S(2)}) copy-start(bf16[3,128,256]{2,1,0:T(8,128)(2,1)} %param.14) | copy-start | bytes 589828
  17.2 73.4 %copy-start.5 = (s32[3,4]{1,0:T(4,128)S(1)}, s32[3,4]{1,0:T(4,128)}, u32[]{:S(2)}) copy-start(s32[3,4]{1,0:T(4,128)} %get-tuple-element.28.tranks) | copy-start | bytes 148 | tf_op jit(solution)/shard_map/cond
  17.2 73.4 %copy-start.7 = (s32[3]{0:T(128)S(1)}, s32[3]{0:T(128)}, u32[]{:S(2)}) copy-start(s32[3]{0:T(128)} %get-tuple-element.29.dranks) | copy-start | bytes 40 | tf_op jit(solution)/shard_map/cond
  90.4 1.1 copy-start.1
  93.4 4.5 %collective-permute-start.2 = (bf16[12,256,256]{2,1,0:T(8,128)(2,1)}, bf16[12,256,256]{2,1,0:T(8,128)(2,1)S(1)}, u32[]{:S(2)}, u32[]{:S(2)}) collective-permute-start(bf16[12,256,256]{2,1,0:T(8,128)(2,1)} %get-tuple-element.64), channel_id=1, source_target_pairs={{16,0},{48,32},{80,64},{112,96},{144,128},{176,160},{208,192},{240... | collective-permute-start | bytes 4718600 | tf_op jit(solution)/shard_map/ppermute | solution.py:109
  94.9 3.0 %copy-start = (bf16[3,512,256]{2,1,0:T(8,128)(2,1)S(1)}, bf16[3,512,256]{2,1,0:T(8,128)(2,1)}, u32[]{:S(2)}) copy-start(bf16[3,512,256]{2,1,0:T(8,128)(2,1)} %ours.1) | copy-start | bytes 2359300
  94.9 3.0 %copy-start.4 = (s32[3,4]{1,0:T(4,128)S(1)}, s32[3,4]{1,0:T(4,128)}, u32[]{:S(2)}) copy-start(s32[3,4]{1,0:T(4,128)} %tranks.1) | copy-start | bytes 148
  94.9 3.0 %copy-start.6 = (s32[3]{0:T(128)S(1)}, s32[3]{0:T(128)}, u32[]{:S(2)}) copy-start(s32[3]{0:T(128)} %dranks.1) | copy-start | bytes 40
  100.9 5.2 %collective-permute-start.3 = (bf16[16,64,512]{2,1,0:T(8,128)(2,1)S(1)}, bf16[16,64,512]{2,1,0:T(8,128)(2,1)S(1)}, u32[]{:S(2)}, u32[]{:S(2)}) collective-permute-start(bf16[16,64,512]{2,1,0:T(8,128)(2,1)S(1)} %bitcast.121), channel_id=1, source_target_pairs={{0,16},{32,48},{64,80},{96,112},{128,144},{160,176},{192,208},{224... | collective-permute-start | bytes 3145736 | tf_op jit(solution)/shard_map/ppermute | solution.py:129
  106.1 22.5 %copy-start.3 = (f32[512,64]{0,1:T(8,128)S(1)}, f32[512,64]{0,1:T(8,128)}, u32[]{:S(2)}) copy-start(f32[512,64]{0,1:T(8,128)} %param.11) | copy-start | bytes 393220
